TPU v7x, 128 devices: a whole 4x4x4 slice. The times are simulated.
128 devices in a mesh: ctx: 16 (over x, z), exp: 8 (over y, core).
Axes of the slice: x: 4, y: 4, z: 4, core: 2. Of those that a mesh axis runs over, the one named last changes fastest.
Arguments:
- residual: bfloat16 [16384, 6400], P(('ctx', 'exp')), may hold values from -6 to 6
- shared_out: bfloat16 [16384, 6400], P(('ctx', 'exp')), may hold values from -6 to 6
- expert_out: bfloat16 [16, 8, 8, 2, 16, 6400], P('ctx', 'exp'), may hold values from -6 to 6
- expert_id: int32 [16384, 1], P(('ctx', 'exp')), may hold values from 0 to 15; in each aligned block of 128 rows (0 to 127, 128 to 255, ...) at most 16 rows name the same one
- gate_value: float32 [16384, 1], P(('ctx', 'exp')), may hold values from 0.3 to 1
- doc_lengths: int32 [32], replicated, may hold values from 1 to 2049, 16384 in all
- norm_gain: float32 [6400], replicated, may hold values from 0.1 to 1.9
- w_query: bfloat16 [6400, 5120], P('ctx', 'exp'), may hold values from -0.078125 to 0.078125
- key_value_weight: bfloat16 [6400, 1024], P('ctx'), may hold values from -0.078125 to 0.078125
- query_gain: float32 [128], replicated, may hold values from 0.5 to 24
- key_gain: float32 [128], replicated, may hold values from 0.5 to 24
Outputs:
- hidden_out: bfloat16 [16384, 6400], P(('ctx', 'exp'))
- attended: bfloat16 [16384, 5120], P('ctx', 'exp')
Inputs may be any that keep to these rules, and one draw needn't show every extreme that they name: `expert_id`: in the rows of one device no expert is named by more than 16 tokens, and some expert by exactly that many. `doc_lengths`: the lengths sum to 16384; the longest is 2049.
All inputs are finite; a program needn't handle non-finite values.
Results may differ from a plain program's by a relative error of at most 0.017.
The roundings to bfloat16 on the way count: a program that leaves them out, or rounds other values in their place, can miss the bound.
Values may be sent and summed in bfloat16 or wider, within the bound.
A program may use at most 192 MiB of HBM per device.

v0:
```python
import jax
import jax.numpy as jnp
from jax import lax
from jax.sharding import PartitionSpec as P

HEAD_DIM = 128
QUERY_HEADS = 40
KEY_VALUE_HEADS = 4
DOC_SHARD_SPAN = 2


eps_value = 1e-06
neg_large = -1e30


def from_behind(value, axis, steps):
    count = lax.axis_size(axis)
    initial, last = (max(0, -steps), min(count, count - steps))
    return lax.ppermute(value, axis, [(source, source + steps) for source in range(initial, last)])


def rms_scale(values_in, gain_vector):
    mean_square = jnp.mean(values_in * values_in, axis=-1, keepdims=True)
    return values_in * lax.rsqrt(mean_square + eps_value) * gain_vector


def document_of(positions, doc_lengths):
    doc_ends = jnp.cumsum(doc_lengths)
    return jnp.sum((doc_ends[None, :] <= positions[:, None]).astype(jnp.int32), axis=1)


def per_device(
    residual,
    shared_out,
    expert_out,
    expert_id,
    gate_value,
    doc_lengths,
    norm_gain,
    w_query,
    key_value_weight,
    query_gain,
    key_gain,
):
    model_width = residual.shape[1]
    held_rows = expert_out.reshape(expert_out.shape[2:])
    returned = lax.all_to_all(held_rows, "exp", split_axis=0, concat_axis=0, tiled=True)
    n_experts = returned.shape[0] * returned.shape[1]
    slots_each = returned.shape[2]
    row_table = returned.reshape(n_experts * slots_each, model_width)
    chosen = expert_id[:, 0]
    onehot = (chosen[:, None] == jnp.arange(n_experts, dtype=jnp.int32)[None, :]).astype(jnp.int32)
    before = jnp.cumsum(onehot, axis=0) - onehot
    slot_index = jnp.sum(onehot * before, axis=1)
    routed_rows = jnp.take(row_table, chosen * slots_each + slot_index, axis=0)
    summed = (
        residual.astype(jnp.float32)
        + shared_out.astype(jnp.float32)
        + gate_value * routed_rows.astype(jnp.float32)
    )
    hidden_out = summed.astype(jnp.bfloat16)
    normed = rms_scale(summed, norm_gain).astype(jnp.bfloat16)
    shard_rows = lax.all_gather(normed, "exp", axis=0, tiled=True)
    shard_len = shard_rows.shape[0]
    exp_index = lax.axis_index("exp")
    ctx_index = lax.axis_index("ctx")
    heads_here = w_query.shape[1] // HEAD_DIM
    query_group_count = QUERY_HEADS // KEY_VALUE_HEADS
    kv_head = exp_index * heads_here // query_group_count
    head_weights = lax.dynamic_slice_in_dim(
        key_value_weight, kv_head * 2 * HEAD_DIM, 2 * HEAD_DIM, 1
    )
    query_raw = jnp.dot(
        shard_rows,
        lax.all_gather(w_query, "ctx", axis=0, tiled=True),
        preferred_element_type=jnp.float32,
    )
    key_value_projected = jnp.dot(
        shard_rows,
        lax.all_gather(head_weights, "ctx", axis=0, tiled=True),
        preferred_element_type=jnp.float32,
    )
    queries = rms_scale(query_raw.reshape(shard_len, heads_here, HEAD_DIM), query_gain).astype(
        jnp.bfloat16
    )
    key_part = rms_scale(key_value_projected[:, :HEAD_DIM], key_gain)
    packed = jnp.concatenate([key_part, key_value_projected[:, HEAD_DIM:]], axis=1).astype(
        jnp.bfloat16
    )
    offsets = jnp.arange(shard_len, dtype=jnp.int32)
    query_pos = ctx_index * shard_len + offsets
    query_doc = document_of(query_pos, doc_lengths)
    score_scale = HEAD_DIM ** (-0.5)

    def absorb(carried, kv_block, distance):
        key_pos = (ctx_index - distance) * shard_len + offsets
        key_doc = document_of(key_pos, doc_lengths)
        allowed = (
            (key_doc[None, :] == query_doc[:, None])
            & (key_pos[None, :] <= query_pos[:, None])
            & (key_pos[None, :] >= 0)
        )

        def update(current):
            run_max, run_sum, weighted = current
            scores = (
                jnp.einsum(
                    "qhd,kd->hqk",
                    queries,
                    kv_block[:, :HEAD_DIM],
                    preferred_element_type=jnp.float32,
                )
                * score_scale
            )
            scores = jnp.where(allowed[None], scores, neg_large)
            new_max = jnp.maximum(run_max, jnp.max(scores, axis=2))
            weights_now = jnp.where(allowed[None], jnp.exp(scores - new_max[..., None]), 0.0)
            factor = jnp.exp(run_max - new_max)
            run_sum = run_sum * factor + jnp.sum(weights_now, axis=2)
            probs = weights_now.astype(jnp.bfloat16)
            weighted = weighted * factor[..., None] + jnp.einsum(
                "hqk,kd->hqd", probs, kv_block[:, HEAD_DIM:], preferred_element_type=jnp.float32
            )
            return (new_max, run_sum, weighted)

        def keep_state(current):
            return current

        return lax.cond(jnp.any(allowed), update, keep_state, carried)

    carried = (
        jnp.full((heads_here, shard_len), neg_large, jnp.float32),
        jnp.zeros((heads_here, shard_len), jnp.float32),
        jnp.zeros((heads_here, shard_len, HEAD_DIM), jnp.float32),
    )
    carried = absorb(carried, packed, 0)
    for distance in range(1, DOC_SHARD_SPAN + 1):
        earlier = from_behind(packed, "ctx", distance)
        carried = absorb(carried, earlier, distance)
    run_max, run_sum, weighted = carried
    finished = weighted / run_sum[..., None]
    attended = (
        jnp.transpose(finished, (1, 0, 2))
        .reshape(shard_len, heads_here * HEAD_DIM)
        .astype(jnp.bfloat16)
    )
    return (hidden_out, attended)


def solution(mesh):
    placed = (
        P(("ctx", "exp"), None),
        P(("ctx", "exp"), None),
        P("ctx", "exp", None, None, None, None),
        P(("ctx", "exp"), None),
        P(("ctx", "exp"), None),
        P(),
        P(),
        P("ctx", "exp"),
        P("ctx", None),
        P(),
        P(),
    )
    return jax.shard_map(
        per_device,
        mesh=mesh,
        in_specs=placed,
        out_specs=(P(("ctx", "exp"), None), P("ctx", "exp")),
        check_vma=False,
    )
```

profile of v0, /device:TPU:65, one launch (start us, length us, event | category | flops | bytes accessed | tf_op | source)
XLA Modules:
  0.0 307.6 jit_solution(4606888027192907856)
XLA Ops:
  7.9 5.2 %all-to-all-start = ((bf16[8,2,16,6400]{3,2,1,0:T(8,128)(2,1)}), bf16[8,2,16,6400]{3,2,1,0:T(8,128)(2,1)}, u32[]{:S(2)}, u32[]{:S(2)}) async-start(bf16[8,2,16,6400]{3,2,1,0:T(8,128)(2,1)} %bitcast.90), calls=%async_computation | async-start | bytes 6553600 | tf_op jit(solution)/shard_map/all_to_all | solution.py:47
  13.6 38.6 %all-to-all-done = bf16[8,2,16,6400]{3,2,1,0:T(8,128)(2,1)} async-done(((bf16[8,2,16,6400]{3,2,1,0:T(8,128)(2,1)}), bf16[8,2,16,6400]{3,2,1,0:T(8,128)(2,1)}, u32[]{:S(2)}, u32[]{:S(2)}) %all-to-all-start) | async-done | bytes 3276832 | tf_op jit(solution)/shard_map/all_to_all | solution.py:47
  52.2 5.5 %gather_fusion = bf16[128,6400]{1,0:T(8,128)(2,1)S(1)} fusion(bf16[256,6400]{1,0:T(8,128)(2,1)} %bitcast.14, s32[1024]{0:T(1024)S(1)} %pad_clamp_fusion), kind=kCustom, calls=%fused_computation | custom fusion | bytes 3277312 | tf_op jit(solution)/shard_map/jit(_take)/gather | solution.py:55
  57.8 3.2 %multiply_reduce_fusion = f32[128]{0:T(128)S(1)} fusion(bf16[128,6400]{1,0:T(8,128)(2,1)S(1)} %gather_fusion, pred[128]{0:T(512)(128)(4,1)S(1)} %get-tuple-element.138, f32[128]{0:T(128)S(1)} %bitcast.93, bf16[128,6400]{1,0:T(8,128)(2,1)} %param.18, bf16[128,6400]{1,0:T(8,128)(2,1)} %param.17), kind=kLoop, calls=%fused_computation.54 | loop fusion | flops 7372672 | bytes 4916352 | tf_op jit(solution)/shard_map/reduce_sum | solution.py:23
  61.0 3.2 %multiply_convert_fusion = (bf16[128,6400]{1,0:T(8,128)(2,1)}, bf16[128,6400]{1,0:T(8,128)(2,1)}) fusion(f32[6400]{0:T(1024)S(1)} %copy-done.9, f32[128]{0:T(128)S(1)} %add_rsqrt_fusion.2, bf16[128,6400]{1,0:T(8,128)(2,1)S(1)} %gather_fusion, pred[128]{0:T(512)(128)(4,1)S(1)} %get-tuple-element.138, f32[128]{0:T(128)S(1)} %bitcast.94, ...), kind=kLoop, calls=%fused_computation.53 | loop fusion | flops 9011200 | bytes 8218752 | tf_op jit(solution)/shard_map/convert_element_type | solution.py:62
  65.7 6.2 %and_and_fusion = (pred[1024,1024]{0,1:T(8,128)(4,1)}, pred[]{:T(512)}, pred[]{:T(512)}, pred[1024,1024]{0,1:T(8,128)(4,1)}, pred[]{:T(512)}, /*index=5*/pred[1024,1024]{0,1:T(8,128)(4,1)}) fusion(s32[1024]{0:T(1024)S(1)} %get-tuple-element.155, s32[1024]{0:T(1024)S(1)} %get-tuple-element.126, pred[1024]{0:T(1024)(128)(4,1)S(1)} %get-tuple-element.156, ...), kind=kLoop, calls=%fused_computation.50 | loop fusion | flops 15728637 | bytes 3173379 | tf_op jit(solution)/shard_map/and | solution.py:99
  74.0 7.8 %all-gather.8.cloned.1.call-done = bf16[6400,640]{1,0:T(8,128)(2,1)} async-done(((bf16[400,640]{1,0:T(8,128)(2,1)}), bf16[6400,640]{1,0:T(8,128)(2,1)}) %all-gather.8.cloned.1.call-update) | async-done | bytes 8192016 | tf_op jit(solution)/shard_map/all_gather | solution.py:75
  81.7 71.5 %all-gather.4.cloned.1.call-done = bf16[1024,6400]{1,0:T(8,128)(2,1)} async-done(((bf16[128,6400]{1,0:T(8,128)(2,1)}), bf16[1024,6400]{1,0:T(8,128)(2,1)}) %all-gather.4.cloned.1.call-update) | async-done | bytes 13107216 | tf_op jit(solution)/shard_map/all_gather | solution.py:63
  153.3 15.3 %fusion.44 = f32[1024,640]{0,1:T(8,128)} fusion(bf16[1024,6400]{1,0:T(8,128)(2,1)} %all-gather.4.cloned.1.call-done, bf16[6400,640]{1,0:T(8,128)(2,1)} %all-gather.8.cloned.1.call-done), kind=kOutput, calls=%fused_computation.88 | convolution fusion | flops 8388608000 | bytes 23920640 | tf_op jit(solution)/shard_map/dot_general | solution.py:73
  168.5 2.1 copy.36
  170.7 2.1 multiply_reduce_fusion.1
  172.8 30.6 %all-gather.6.cloned.1.call-done = bf16[6400,256]{1,0:T(8,128)(2,1)} async-done(((bf16[400,256]{1,0:T(8,128)(2,1)}), bf16[6400,256]{1,0:T(8,128)(2,1)}) %all-gather.6.cloned.1.call-update) | async-done | bytes 3276816 | tf_op jit(solution)/shard_map/all_gather | solution.py:80
  203.3 7.6 %fusion.43 = f32[1024,256]{0,1:T(8,128)S(1)} fusion(bf16[1024,6400]{1,0:T(8,128)(2,1)} %all-gather.4.cloned.1.call-done, bf16[6400,256]{1,0:T(8,128)(2,1)} %all-gather.6.cloned.1.call-done), kind=kOutput, calls=%fused_computation.87 | convolution fusion | flops 3355443200 | bytes 17432576 | tf_op jit(solution)/shard_map/dot_general | solution.py:78
  212.0 3.2 %collective-permute-start.1 = (bf16[1024,256]{0,1:T(8,128)(2,1)}, bf16[1024,256]{0,1:T(8,128)(2,1)}, u32[]{:S(2)}, u32[]{:S(2)}) collective-permute-start(bf16[1024,256]{0,1:T(8,128)(2,1)} %pad_maximum_fusion), channel_id=1, source_target_pairs={{0,16},{8,24},{16,32},{24,40},{32,48},{40,56},{48,64},{56,72},{64,... | collective-permute-start | bytes 1572872 | tf_op jit(solution)/shard_map/ppermute | solution.py:19
  215.2 2.4 collective-permute-start
  217.7 1.7 multiply_convert_fusion.1
  219.3 23.0 %conditional.3 = (f32[5,1024]{1,0:T(8,128)}, f32[5,1024]{1,0:T(8,128)S(1)}, f32[5,1024,128]{2,1,0:T(8,128)}) conditional(s32[]{:T(128)} %convert_element_type.69, () %tuple.29, (pred[1024,1024]{0,1:T(8,128)(4,1)}, bf16[1024,256]{0,1:T(8,128)(2,1)}, bf16[1024,5,128]{2,0,1:T(8,128)(2,1)}) %tuple.30), branch_computations={%region_12.13_spmd, %region_13.16_spmd} | conditional | flops 2753187840 | bytes 75997240 | solution.py:129
  220.6 5.2 %fusion = (f32[5,1024]{1,0:T(8,128)S(1)}, f32[1024,1024,5]{1,0,2:T(8,128)S(1)}) fusion(pred[1024,1024]{0,1:T(8,128)(4,1)} %get-tuple-element.40, bf16[1024,5,128]{2,0,1:T(8,128)(2,1)} %get-tuple-element.42, bf16[1024,256]{1,0:T(8,128)(2,1)S(1)} %copy.37), kind=kOutput, calls=%fused_computation.3 | convolution fusion | flops 1357900800 | bytes 23613440 | tf_op jit(solution)/shard_map/cond/branch_1_fun/qhd,kd->hqk/dot_general | solution.py:107
  226.4 6.2 %fusion.2 = f32[5,1024]{1,0:T(8,128)S(1)} fusion(f32[1024,1024,5]{1,0,2:T(8,128)S(1)} %get-tuple-element.141, f32[5,1024]{1,0:T(8,128)} %get-tuple-element.161, pred[1024,1024]{0,1:T(8,128)(4,1)S(1)} %copy-done.6), kind=kLoop, calls=%fused_computation.5 | loop fusion | flops 26209280 | bytes 22061056 | tf_op jit(solution)/shard_map/cond/branch_1_fun/reduce_sum | solution.py:119
  232.6 8.9 %fusion.6 = f32[5,1024,128]{2,1,0:T(8,128)} fusion(f32[1024,1024,5]{1,0,2:T(8,128)S(1)} %get-tuple-element.141, f32[5,1024]{1,0:T(8,128)} %get-tuple-element.161, pred[1024,1024]{0,1:T(8,128)(4,1)} %get-tuple-element.40, f32[5,1024]{1,0:T(8,128)S(1)} %get-tuple-element.128, bf16[1024,256]{1,0:T(8,128)(2,1)S(1)} %copy.37), kind=kOutput, calls=%fused_computation.8 | convolution fusion | flops 1369047040 | bytes 24956928 | tf_op jit(solution)/shard_map/cond/branch_1_fun/hqk,kd->hqd/dot_general | solution.py:121
  242.3 26.9 %conditional.4 = ((f32[5,1024]{1,0:T(8,128)}, f32[5,1024]{1,0:T(8,128)S(1)}, f32[5,1024,128]{2,1,0:T(8,128)})) conditional(s32[]{:T(128)} %convert_element_type.68, (f32[5,1024]{1,0:T(8,128)}, f32[5,1024]{1,0:T(8,128)S(1)}, f32[5,1024,128]{2,1,0:T(8,128)}) %conditional.3, (pred[1024,1024]{0,1:T(8,128)(4,1)}, bf16[1024,256]{0,1:T(8,128)(2,1)}, ...), branch_computations={%region_16.17_spmd, %region_17.20_spmd} | conditional | flops 2753832960 | bytes 162619488 | solution.py:129
  242.4 1.3 copy.38
  243.7 5.2 %fusion.14 = (f32[5,1024]{1,0:T(8,128)S(1)}, f32[1024,1024,5]{1,0,2:T(8,128)S(1)}) fusion(pred[1024,1024]{0,1:T(8,128)(4,1)} %get-tuple-element.44, bf16[1024,5,128]{2,0,1:T(8,128)(2,1)} %get-tuple-element.46, bf16[1024,256]{1,0:T(8,128)(2,1)S(1)} %copy.38), kind=kOutput, calls=%fused_computation.20 | convolution fusion | flops 1357900800 | bytes 23613440 | tf_op jit(solution)/shard_map/cond/branch_1_fun/qhd,kd->hqk/dot_general | solution.py:107
  249.7 5.4 %fusion.16 = f32[5,1024]{1,0:T(8,128)S(1)} fusion(f32[1024,1024,5]{1,0,2:T(8,128)S(1)} %get-tuple-element.143, f32[5,1024]{1,0:T(8,128)S(1)} %max.4, pred[1024,1024]{0,1:T(8,128)(4,1)S(1)} %copy-done.5), kind=kLoop, calls=%fused_computation.22 | loop fusion | flops 26209280 | bytes 22061056 | tf_op jit(solution)/shard_map/cond/branch_1_fun/reduce_sum | solution.py:119
  256.6 12.0 %multiply_add_fusion = f32[5,1024,128]{2,1,0:T(8,128)} fusion(f32[5,1024,128]{2,1,0:T(8,128)} %get-tuple-element.48, f32[1024,1024,5]{1,0,2:T(8,128)} %copy-done.2, f32[5,1024]{1,0:T(8,128)S(1)} %max.4, pred[1024,1024]{0,1:T(8,128)(4,1)S(1)} %copy-done.5, f32[5,1024]{1,0:T(8,128)S(1)} %get-tuple-element.131, bf16[1024,256]{1,0:T(8,128)(2,1)S(1)} %copy.38), kind=kOutput, calls=%fused_computation.25 | convolution fusion | flops 1369702400 | bytes 27590656 | tf_op jit(solution)/shard_map/cond/branch_1_fun/hqk,kd->hqd/dot_general | solution.py:121
  269.2 28.0 %conditional.5 = (f32[5,1024]{1,0:T(8,128)S(1)}, f32[5,1024,128]{1,2,0:T(8,128)S(1)}) conditional(s32[]{:T(128)} %convert_element_type.66, (f32[5,1024]{1,0:T(8,128)S(1)}, f32[5,1024,128]{2,1,0:T(8,128)}) %tuple.32, (pred[1024,1024]{0,1:T(8,128)(4,1)S(1)}, bf16[1024,256]{0,1:T(8,128)(2,1)}, bf16[1024,5,128]{2,0,1:T(8,128)(2,1)}, ...), branch_computations={%region_20.21_spmd, %region_21.24_spmd} | conditional | flops 2753832960 | bytes 163627056 | solution.py:129
  270.5 4.9 %fusion.26 = (f32[5,1024]{1,0:T(8,128)S(1)}, f32[1024,1024,5]{1,0,2:T(8,128)S(1)}) fusion(pred[1024,1024]{0,1:T(8,128)(4,1)S(1)} %get-tuple-element.51, bf16[1024,5,128]{2,0,1:T(8,128)(2,1)} %get-tuple-element.53, bf16[1024,256]{1,0:T(8,128)(2,1)S(1)} %copy.39), kind=kOutput, calls=%fused_computation.36 | convolution fusion | flops 1357900800 | bytes 23613440 | tf_op jit(solution)/shard_map/cond/branch_1_fun/qhd,kd->hqk/dot_general | solution.py:107
  276.2 5.4 %fusion.28 = f32[5,1024]{1,0:T(8,128)S(1)} fusion(f32[1024,1024,5]{1,0,2:T(8,128)S(1)} %get-tuple-element.145, f32[5,1024]{1,0:T(8,128)S(1)} %max.5, pred[1024,1024]{0,1:T(8,128)(4,1)S(1)} %get-tuple-element.51), kind=kLoop, calls=%fused_computation.38 | loop fusion | flops 26209280 | bytes 22061056 | tf_op jit(solution)/shard_map/cond/branch_1_fun/reduce_sum | solution.py:119
  283.1 12.0 %multiply_add_fusion.2 = f32[5,1024,128]{2,1,0:T(8,128)} fusion(f32[5,1024,128]{2,1,0:T(8,128)} %get-tuple-element.54, f32[1024,1024,5]{1,0,2:T(8,128)} %copy-done.3, f32[5,1024]{1,0:T(8,128)S(1)} %max.5, pred[1024,1024]{0,1:T(8,128)(4,1)S(1)} %get-tuple-element.51, f32[5,1024]{1,0:T(8,128)S(1)} %get-tuple-element.133, bf16[1024,256]{1,0:T(8,128)(2,1)S(1)} %copy.39), kind=kOutput, calls=%fused_computation.41 | convolution fusion | flops 1369702400 | bytes 27590656 | tf_op jit(solution)/shard_map/cond/branch_1_fun/hqk,kd->hqd/dot_general | solution.py:121
  295.1 2.2 copy.46
  297.3 1.4 divide_convert_fusion
  298.7 2.4 copy.41
  (68 shorter events, 12.8 us)
Async XLA Ops:
  7.2 57.4 %copy-start = (bf16[400,1024]{1,0:T(8,128)(2,1)S(1)}, bf16[400,1024]{1,0:T(8,128)(2,1)}, u32[]{:S(2)}) copy-start(bf16[400,1024]{1,0:T(8,128)(2,1)} %param.25) | copy-start | bytes 2457604
  7.2 5.9 %copy-start.10 = (s32[128,1]{0,1:T(1,128)S(1)}, s32[128,1]{0,1:T(1,128)}, u32[]{:S(2)}) copy-start(s32[128,1]{0,1:T(1,128)} %param.20) | copy-start | bytes 1540
  7.2 74.5 %all-gather.8.cloned.1.call-start = ((), (), s32[]{:S(2)}) async-start(), calls=%async_computation.3 | async-start | bytes 8704000 | tf_op jit(solution)/shard_map/all_gather | solution.py:75
  7.9 44.2 %all-to-all-start = ((bf16[8,2,16,6400]{3,2,1,0:T(8,128)(2,1)}), bf16[8,2,16,6400]{3,2,1,0:T(8,128)(2,1)}, u32[]{:S(2)}, u32[]{:S(2)}) async-start(bf16[8,2,16,6400]{3,2,1,0:T(8,128)(2,1)} %bitcast.90), calls=%async_computation | async-start | bytes 6553600 | tf_op jit(solution)/shard_map/all_to_all | solution.py:47
  13.1 140.2 %all-gather.4.cloned.1.call-start = ((), (), s32[]{:S(2)}) async-start(), calls=%async_computation.1 | async-start | bytes 14745600 | tf_op jit(solution)/shard_map/all_gather | solution.py:63
  52.2 5.6 %copy-start.11 = (f32[128,1]{0,1:T(1,128)S(1)}, f32[128,1]{0,1:T(1,128)}, u32[]{:S(2)}) copy-start(f32[128,1]{0,1:T(1,128)} %param.21) | copy-start | bytes 1540
  52.2 8.8 %copy-start.9 = (f32[6400]{0:T(1024)S(1)}, f32[6400]{0:T(1024)}, u32[]{:S(2)}) copy-start(f32[6400]{0:T(1024)} %param.23) | copy-start | bytes 76804
  57.7 3.3 %copy-start.7 = (bf16[128,6400]{1,0:T(8,128)(2,1)S(1)}, bf16[128,6400]{1,0:T(8,128)(2,1)}, u32[]{:S(2)}) copy-start(bf16[128,6400]{1,0:T(8,128)(2,1)} %param.18) | copy-start | bytes 4915204
  57.7 3.3 %copy-start.8 = (bf16[128,6400]{1,0:T(8,128)(2,1)S(1)}, bf16[128,6400]{1,0:T(8,128)(2,1)}, u32[]{:S(2)}) copy-start(bf16[128,6400]{1,0:T(8,128)(2,1)} %param.17) | copy-start | bytes 4915204
  61.0 4.3 %copy-start.13 = (s32[32]{0:T(128)S(1)}, s32[32]{0:T(128)}, u32[]{:S(2)}) copy-start(s32[32]{0:T(128)} %param.22) | copy-start | bytes 388
  64.3 139.1 %all-gather.6.cloned.1.call-start = ((), (), s32[]{:S(2)}) async-start(), calls=%async_computation.2 | async-start | bytes 3481600 | tf_op jit(solution)/shard_map/all_gather | solution.py:80
  172.7 38.3 %copy-start.14 = (f32[128]{0:T(128)S(1)}, f32[128]{0:T(128)}, u32[]{:S(2)}) copy-start(f32[128]{0:T(128)} %param.27) | copy-start | bytes 1540
  172.8 44.9 %copy-start.12 = (f32[128]{0:T(128)S(1)}, f32[128]{0:T(128)}, u32[]{:S(2)}) copy-start(f32[128]{0:T(128)} %param.26) | copy-start | bytes 1540
  212.0 57.2 %collective-permute-start.1 = (bf16[1024,256]{0,1:T(8,128)(2,1)}, bf16[1024,256]{0,1:T(8,128)(2,1)}, u32[]{:S(2)}, u32[]{:S(2)}) collective-permute-start(bf16[1024,256]{0,1:T(8,128)(2,1)} %pad_maximum_fusion), channel_id=1, source_target_pairs={{0,16},{8,24},{16,32},{24,40},{32,48},{40,56},{48,64},{56,72},{64,... | collective-permute-start | bytes 1572872 | tf_op jit(solution)/shard_map/ppermute | solution.py:19
  215.2 27.1 %collective-permute-start = (bf16[1024,256]{0,1:T(8,128)(2,1)}, bf16[1024,256]{0,1:T(8,128)(2,1)}, u32[]{:S(2)}, u32[]{:S(2)}) collective-permute-start(bf16[1024,256]{0,1:T(8,128)(2,1)} %pad_maximum_fusion), channel_id=1, source_target_pairs={{0,8},{8,16},{16,24},{24,32},{32,40},{40,48},{48,56},{56,64},{64,7... | collective-permute-start | bytes 1572872 | tf_op jit(solution)/shard_map/ppermute | solution.py:19
  220.6 5.8 %copy-start.6 = (pred[1024,1024]{0,1:T(8,128)(4,1)S(1)}, pred[1024,1024]{0,1:T(8,128)(4,1)}, u32[]{:S(2)}) copy-start(pred[1024,1024]{0,1:T(8,128)(4,1)} %get-tuple-element.40) | copy-start | bytes 3145732 | tf_op jit(solution)/shard_map/cond
  242.3 26.9 %copy-start.4 = (pred[1024,1024]{0,1:T(8,128)(4,1)S(1)}, pred[1024,1024]{0,1:T(8,128)(4,1)}, u32[]{:S(2)}) copy-start(pred[1024,1024]{0,1:T(8,128)(4,1)} %get-tuple-element.153) | copy-start | bytes 3145732
  243.7 6.0 %copy-start.5 = (pred[1024,1024]{0,1:T(8,128)(4,1)S(1)}, pred[1024,1024]{0,1:T(8,128)(4,1)}, u32[]{:S(2)}) copy-start(pred[1024,1024]{0,1:T(8,128)(4,1)} %get-tuple-element.44) | copy-start | bytes 3145732 | tf_op jit(solution)/shard_map/cond
  248.9 7.0 %copy-start.2 = (f32[1024,1024,5]{1,0,2:T(8,128)}, f32[1024,1024,5]{1,0,2:T(8,128)S(1)}, u32[]{:S(2)}) copy-start(f32[1024,1024,5]{1,0,2:T(8,128)S(1)} %get-tuple-element.143) | copy-start | bytes 62914564 | tf_op jit(solution)/shard_map/cond
  275.4 7.0 %copy-start.3 = (f32[1024,1024,5]{1,0,2:T(8,128)}, f32[1024,1024,5]{1,0,2:T(8,128)S(1)}, u32[]{:S(2)}) copy-start(f32[1024,1024,5]{1,0,2:T(8,128)S(1)} %get-tuple-element.145) | copy-start | bytes 62914564 | tf_op jit(solution)/shard_map/cond
  297.3 3.9 %copy-start.1 = (bf16[400,1024]{1,0:T(8,128)(2,1)S(1)}, bf16[400,1024]{1,0:T(8,128)(2,1)}, u32[]{:S(2)}) copy-start(bf16[400,1024]{1,0:T(8,128)(2,1)} %param.25) | copy-start | bytes 2457604
Sparse Core Ops, SparseCore 0:
  10.2 71.4 all-gather.7
  83.4 69.8 all-gather.3
  156.0 47.2 all-gather.5
where the time goes:
time: 309 us; the launch traced here: 308 us
  waiting for transfers between devices  149 us (48%)
  matrix products  71 us (23%)
  other arithmetic  41.2 us (13%)
  local copies, waits for them, and re-layouts  19.1 us (6%)
  between operations  16.1 us (5%)
  starting transfers between devices  11 us (4%)
    all_gather x1, waiting for transfers between devices, per_device(): shard_rows = lax.all_gather(normed, 'exp', axis=0, tiled=True)  71.5 us
    all_to_all x1, waiting for transfers between devices, per_device(): lax.all_to_all(held_rows, 'exp', split_axis=0, concat_axis=0, tiled=True)  38.6 us
    dot_general x3, matrix products, update(): jnp.einsum('hqk,kd->hqd', probs, kv_block[:, HEAD_DIM:], preferred_elemen...  32.8 us
    all_gather x1, waiting for transfers between devices, per_device(): lax.all_gather(head_weights, 'ctx', axis=0, tiled=True)  30.6 us
    reduce_sum x3, other arithmetic, update(): run_sum = run_sum * factor + jnp.sum(weights_now, axis=2)  17.1 us
    dot_general x1, matrix products, per_device(): jnp.dot(shard_rows, lax.all_gather(w_query, 'ctx', axis=0, tiled=True), p...  15.3 us
    dot_general x3, matrix products, update(): jnp.einsum('qhd,kd->hqk', queries, kv_block[:, :HEAD_DIM], preferred_elem...  15.3 us
    all_gather x1, waiting for transfers between devices, per_device(): lax.all_gather(w_query, 'ctx', axis=0, tiled=True)  7.76 us
  transfers between devices with their start and end apart: 6, of which 4 were waited for; matrix products, arithmetic and copies ran while one was open for 29% of the time, Pallas kernels for 0%

commit v1 on v0

v1 whole, which is shorter than its diff:
```python
import functools
import math

import jax
import jax.numpy as jnp
from jax import lax
from jax.experimental import pallas as pl
from jax.experimental.pallas import tpu as pltpu
from jax.sharding import PartitionSpec as P

MESH = pl.DeviceIdType.MESH
MODEL = 6400
HEAD = 128
HEADS = 5
COLS = (HEADS + 1) * HEAD
TOK = 128
SHARD = 1024
N_CTX = 16
N_EXP = 8
SLOTS = 32
FCH = 5
FW = MODEL // FCH
PCH = 4
PR = TOK // PCH
PM = N_EXP * PR
WROWS = 400
WA = 208
WB = WROWS - WA
EPS = 1e-06
VMEM_LIMIT = 56 * 1024 * 1024


def rms_rows(values, gain):
    mean_square = jnp.mean(values * values, axis=-1, keepdims=True)
    return values * lax.rsqrt(mean_square + EPS) * gain


def exchange_kernel(
    res_hbm, sh_hbm, ex_hbm, eid_ref, gate_ref, gain_ref, wq_hbm, wkv_hbm, qg_ref, kg_ref,
    hid_hbm, q_hbm, kv_hbm,
    slots, res, sh, summed, hid, xall, wall, qbuf, kvbuf,
    loc_sem, a_send, a_recv, a_own, w_send, w_recv1, w_recv2, x_send, x_recv, s_send, s_recv,
    h_send, h_recv, hs_send, hs_recv, out_sem,
):
    c = lax.axis_index("ctx")
    e = lax.axis_index("exp")
    x, z = c // 4, c % 4
    y, k = e // 2, e % 2

    def along_x(d):
        return (((x + d) % 4) * 4 + z, e)

    def along_z(d):
        return (x * 4 + (z + d) % 4, e)

    def along_y(d):
        return (c, ((y + d) % 4) * 2 + k)

    def along_ctx(d):
        return ((c + d + N_CTX) % N_CTX, e)

    sibling = (c, y * 2 + (1 - k))

    def remote(src, dst, send, recv, to):
        pltpu.make_async_remote_copy(
            src_ref=src, dst_ref=dst, send_sem=send, recv_sem=recv, device_id=to, device_id_type=MESH
        ).start()

    def done(ref, sem):
        pltpu.make_async_copy(ref, ref, sem).wait()

    w_own = wall.at[pl.ds(pl.multiple_of(c * WROWS, 16), WROWS), :]
    load_q = pltpu.make_async_copy(wq_hbm, w_own.at[:, : HEADS * HEAD], loc_sem.at[0])
    load_q.start()
    kv_column = pl.multiple_of(e * HEAD, HEAD)
    load_kv = pltpu.make_async_copy(
        wkv_hbm.at[:, pl.ds(kv_column, HEAD)], w_own.at[:, HEADS * HEAD :], loc_sem.at[1]
    )
    load_kv.start()
    load_res = pltpu.make_async_copy(res_hbm, res, loc_sem.at[2])
    load_res.start()
    load_sh = pltpu.make_async_copy(sh_hbm, sh, loc_sem.at[3])
    load_sh.start()
    mine = pl.ds(pl.multiple_of(e * SLOTS, SLOTS), SLOTS)
    for f in range(FCH):
        pltpu.make_async_copy(
            ex_hbm.at[e, :, pl.ds(f * FW, FW)], slots.at[f, mine, :], a_own.at[f]
        ).start()

    barrier = pltpu.get_barrier_semaphore()
    for d in range(1, N_EXP):
        pl.semaphore_signal(barrier, inc=1, device_id=(c, (e + d) % N_EXP), device_id_type=MESH)
    for d in range(1, 4):
        pl.semaphore_signal(barrier, inc=1, device_id=along_x(d), device_id_type=MESH)
        pl.semaphore_signal(barrier, inc=1, device_id=along_z(d), device_id_type=MESH)
    for d in (-2, -1, 1, 2):
        pl.semaphore_signal(barrier, inc=1, device_id=along_ctx(d), device_id_type=MESH)
    pl.semaphore_wait(barrier, (N_EXP - 1) + 6 + 4)

    @pl.loop(0, FCH)
    def _(f):
        columns = pl.ds(pl.multiple_of(f * FW, 128), FW)
        for d in range(1, N_EXP):
            to = (e + d) % N_EXP
            remote(ex_hbm.at[to, :, columns], slots.at[f, mine, :], a_send, a_recv.at[f], (c, to))

    def half_a(index):
        return wall.at[pl.ds(pl.multiple_of(index * WROWS, 16), WA), :]

    def half_b(index):
        return wall.at[pl.ds(pl.multiple_of(index * WROWS + WA, 16), WB), :]

    load_q.wait()
    load_kv.wait()
    for d in (1, 3, 2):
        remote(half_a(c), half_a(c), w_send.at[0], w_recv1.at[0, d], along_x(d))
        remote(half_b(c), half_b(c), w_send.at[1], w_recv1.at[1, d], along_z(d))
    for d in (1, 3, 2):
        remote(half_a(c), half_a(c), w_send.at[0], w_recv2.at[0], along_z(d))
        remote(half_b(c), half_b(c), w_send.at[1], w_recv2.at[1], along_x(d))

    experts = 2 * N_EXP
    chosen = eid_ref[...]
    named = chosen == lax.broadcasted_iota(jnp.int32, (TOK, experts), 1)
    named = jnp.where(named, 1.0, 0.0)
    earlier = lax.broadcasted_iota(jnp.int32, (TOK, TOK), 1) < lax.broadcasted_iota(
        jnp.int32, (TOK, TOK), 0
    )
    before = jnp.dot(
        jnp.where(earlier, 1.0, 0.0).astype(jnp.bfloat16),
        named.astype(jnp.bfloat16),
        preferred_element_type=jnp.float32,
    )
    slot = jnp.sum(named * before, axis=1, keepdims=True)
    row = chosen.astype(jnp.float32) * float(SLOTS // 2) + slot
    lane = lax.broadcasted_iota(jnp.int32, (TOK, N_EXP * SLOTS), 1).astype(jnp.float32)
    pick = jnp.where(lane == row, 1.0, 0.0).astype(jnp.bfloat16)
    gate = gate_ref[...]

    for d in (1, 3, 2):
        done(half_a(0), w_recv1.at[0, d])
        got = ((x - d + 4) % 4) * 4 + z
        for d2 in (1, 3, 2):
            remote(half_a(got), half_a(got), w_send.at[0], w_recv2.at[0], along_z(d2))
        done(half_b(0), w_recv1.at[1, d])
        got = x * 4 + (z - d + 4) % 4
        for d2 in (1, 3, 2):
            remote(half_b(got), half_b(got), w_send.at[1], w_recv2.at[1], along_x(d2))

    load_res.wait()
    load_sh.wait()
    squares = jnp.zeros((TOK, 1), jnp.float32)
    for f in range(FCH):
        done(slots.at[f, pl.ds(0, SLOTS), :], a_own.at[f])
        done(slots.at[f, pl.ds(0, SLOTS * (N_EXP - 1)), :], a_recv.at[f])
        columns = pl.ds(f * FW, FW)
        routed = jnp.dot(pick, slots[f], preferred_element_type=jnp.float32)
        total = (
            res[:, columns].astype(jnp.float32) + sh[:, columns].astype(jnp.float32) + gate * routed
        )
        hid[:, columns] = total.astype(jnp.bfloat16)
        summed[:, columns] = total
        squares = squares + jnp.sum(total * total, axis=1, keepdims=True)
    scale = lax.rsqrt(squares * (1.0 / MODEL) + EPS)
    here = pl.ds(pl.multiple_of(e * PR, PR), PR)
    gain = gain_ref[...]
    for p in range(PCH):
        rows = slice(p * PR, (p + 1) * PR)
        xall[p, here, :] = (summed[rows, :] * scale[rows] * gain).astype(jnp.bfloat16)
        block = xall.at[p, here, :]
        for d in (1, 3, 2):
            remote(block, block, x_send, x_recv.at[p, d], along_y(d))
        remote(block, block, s_send, s_recv.at[p], sibling)
    store_hid = pltpu.make_async_copy(hid, hid_hbm, out_sem.at[0])
    store_hid.start()

    done(wall.at[pl.ds(0, 12 * WA), :], w_recv2.at[0])
    done(wall.at[pl.ds(0, 12 * WB), :], w_recv2.at[1])

    def pass_halo(p):
        for dist in (1, 2):
            part = kv_hbm.at[2 - dist, k, :, p]
            done(part, h_recv.at[p, dist])
            remote(part, part, hs_send, hs_recv, sibling)

    @pl.loop(0, PCH)
    def _(p):
        for d in (1, 3, 2):
            source = ((y - d + 4) % 4) * 2 + k
            block = xall.at[p, pl.ds(pl.multiple_of(source * PR, PR), PR), :]
            done(block, x_recv.at[p, d])
            remote(block, block, s_send, s_recv.at[p], sibling)
        done(xall.at[p, pl.ds(0, 4 * PR), :], s_recv.at[p])

        last = jnp.dot(
            xall[p], wall[:, (HEADS - 1) * HEAD :], preferred_element_type=jnp.float32
        )
        raw = last[:, HEAD:]
        part = jnp.where(k == 0, rms_rows(raw, kg_ref[...]), raw).astype(jnp.bfloat16)
        kvbuf[p] = part.reshape(N_EXP, PR, HEAD)
        for dist in (1, 2):
            remote(
                kvbuf.at[p], kv_hbm.at[2 - dist, k, :, p], h_send, h_recv.at[p, dist], along_ctx(dist)
            )
        remote(kvbuf.at[p], kv_hbm.at[2, k, :, p], hs_send, hs_recv, sibling)
        pltpu.make_async_copy(kvbuf.at[p], kv_hbm.at[2, k, :, p], out_sem.at[1]).start()
        head = rms_rows(last[:, :HEAD], qg_ref[...]).astype(jnp.bfloat16)
        qbuf[p, :, :, (HEADS - 1) * HEAD :] = head.reshape(N_EXP, PR, HEAD)
        for pair in range((HEADS - 1) // 2):
            low = pair * 2 * HEAD
            raw = jnp.dot(
                xall[p], wall[:, low : low + 2 * HEAD], preferred_element_type=jnp.float32
            )
            for i in range(2):
                head = rms_rows(raw[:, i * HEAD : (i + 1) * HEAD], qg_ref[...]).astype(jnp.bfloat16)
                qbuf[p, :, :, low + i * HEAD : low + (i + 1) * HEAD] = head.reshape(N_EXP, PR, HEAD)
        pltpu.make_async_copy(qbuf.at[p], q_hbm.at[:, p], out_sem.at[2]).start()

        @pl.when(p > 0)
        def _():
            pass_halo(p - 1)

    pass_halo(PCH - 1)

    done(ex_hbm.at[pl.ds(0, N_EXP - 1)], a_send)
    done(wall.at[pl.ds(0, 15 * WA), :], w_send.at[0])
    done(wall.at[pl.ds(0, 15 * WB), :], w_send.at[1])
    done(xall.at[:, pl.ds(0, 3 * PR), :], x_send)
    done(xall.at[:, pl.ds(0, 4 * PR), :], s_send)
    done(kv_hbm.at[pl.ds(0, 2), 0], h_send)
    done(kv_hbm.at[:, 0], hs_send)
    done(kv_hbm.at[:, 0], hs_recv)
    store_hid.wait()
    done(kv_hbm.at[0, 0], out_sem.at[1])
    done(q_hbm, out_sem.at[2])


def exchange(residual, shared_out, expert_rows, expert_id, gate, gain, w_query, w_kv, q_gain, k_gain):
    any_space = pl.BlockSpec(memory_space=pl.ANY)
    vmem = pl.BlockSpec(memory_space=pltpu.VMEM)
    dma = pltpu.SemaphoreType.DMA
    bf16, f32 = jnp.bfloat16, jnp.float32
    return pl.pallas_call(
        exchange_kernel,
        out_shape=(
            jax.ShapeDtypeStruct((TOK, MODEL), bf16),
            jax.ShapeDtypeStruct((N_EXP, PCH, PR, HEADS * HEAD), bf16),
            jax.ShapeDtypeStruct((3, 2, N_EXP, PCH, PR, HEAD), bf16),
        ),
        in_specs=[any_space] * 3 + [vmem] * 3 + [any_space] * 2 + [vmem] * 2,
        out_specs=(any_space, any_space, any_space),
        scratch_shapes=[
            pltpu.VMEM((FCH, N_EXP * SLOTS, FW), bf16),
            pltpu.VMEM((TOK, MODEL), bf16),
            pltpu.VMEM((TOK, MODEL), bf16),
            pltpu.VMEM((TOK, MODEL), f32),
            pltpu.VMEM((TOK, MODEL), bf16),
            pltpu.VMEM((PCH, PM, MODEL), bf16),
            pltpu.VMEM((MODEL, COLS), bf16),
            pltpu.VMEM((PCH, N_EXP, PR, HEADS * HEAD), bf16),
            pltpu.VMEM((PCH, N_EXP, PR, HEAD), bf16),
            dma((4,)),
            dma,
            dma((FCH,)),
            dma((FCH,)),
            dma((2,)),
            dma((2, 4)),
            dma((2,)),
            dma,
            dma((PCH, 4)),
            dma,
            dma((PCH,)),
            dma,
            dma((PCH, 3)),
            dma,
            dma,
            dma((3,)),
        ],
        compiler_params=pltpu.CompilerParams(
            collective_id=0, has_side_effects=True, vmem_limit_bytes=VMEM_LIMIT
        ),
        cost_estimate=pl.CostEstimate(
            flops=2 * SHARD * MODEL * COLS, bytes_accessed=16 * 1024 * 1024, transcendentals=0
        ),
        name="exchange",
    )(residual, shared_out, expert_rows, expert_id, gate, gain, w_query, w_kv, q_gain, k_gain)


BQ = 256
BK = 256
NEG = -1e30
LOG2E = math.log2(math.e)


def attention_kernel(
    doc_ref, q_ref, kv_ref, hid_hbm, out_ref, hid_out_hbm, vt, m_ref, l_ref, acc_ref, sem
):
    c = lax.axis_index("ctx")
    copy = pltpu.make_async_copy(hid_hbm, hid_out_hbm, sem)
    copy.start()
    window = c * SHARD - 2 * SHARD
    span = 3 * SHARD
    for part in range(3):
        vt[:, part * SHARD : (part + 1) * SHARD] = kv_ref[part, 1].T

    factor = HEAD ** (-0.5) * LOG2E

    @pl.loop(0, SHARD // BQ)
    def _(qb):
        q_low = 2 * SHARD + qb * BQ
        q_rows = pl.ds(pl.multiple_of(qb * BQ, BQ), BQ)
        position = q_low + lax.broadcasted_iota(jnp.int32, (1, BQ), 1)

        def starts(i, carried):
            end, first, least = carried
            end = end + doc_ref[i]
            first = jnp.where(end <= position, end, first)
            return end, first, jnp.where(end <= q_low, end, least)

        _, first, least = lax.fori_loop(
            0, doc_ref.shape[0], starts,
            (0 - window, jnp.zeros((1, BQ), jnp.int32) - window, 0 - window),
        )
        m_ref[...] = jnp.full(m_ref.shape, NEG, jnp.float32)
        l_ref[...] = jnp.zeros(l_ref.shape, jnp.float32)
        acc_ref[...] = jnp.zeros(acc_ref.shape, jnp.float32)

        def block(kb, carried):
            k_low = pl.multiple_of(kb * BK, BK)
            keys = kv_ref.at[kb // (SHARD // BK), 0][
                pl.ds(pl.multiple_of((kb % (SHARD // BK)) * BK, BK), BK), :
            ]
            values = vt[:, pl.ds(k_low, BK)]
            k_position = k_low + lax.broadcasted_iota(jnp.int32, (BK, 1), 0)
            allowed = (k_position >= first) & (k_position <= position)
            for h in range(HEADS):
                scores = lax.dot_general(
                    keys, q_ref[q_rows, h * HEAD : (h + 1) * HEAD], (((1,), (1,)), ((), ())),
                    preferred_element_type=jnp.float32,
                )
                scores = jnp.where(allowed, scores * factor, NEG)
                old = m_ref[h : h + 1, :]
                new = jnp.maximum(old, jnp.max(scores, axis=0, keepdims=True))
                weights = jnp.where(allowed, jnp.exp2(scores - new), 0.0)
                shrink = jnp.exp2(old - new)
                m_ref[h : h + 1, :] = new
                l_ref[h : h + 1, :] = l_ref[h : h + 1, :] * shrink + jnp.sum(
                    weights, axis=0, keepdims=True
                )
                acc_ref[h] = acc_ref[h] * shrink + jnp.dot(
                    values, weights.astype(jnp.bfloat16), preferred_element_type=jnp.float32
                )
            return carried

        lax.fori_loop(least // BK, (q_low + BQ) // BK, block, 0)
        for h in range(HEADS):
            finished = acc_ref[h] / l_ref[h : h + 1, :]
            out_ref[q_rows, h * HEAD : (h + 1) * HEAD] = finished.T.astype(jnp.bfloat16)

    copy.wait()


def attention(doc_lengths, queries, kv, hidden):
    vmem = pl.BlockSpec(memory_space=pltpu.VMEM)
    any_space = pl.BlockSpec(memory_space=pl.ANY)
    return pl.pallas_call(
        attention_kernel,
        out_shape=(
            jax.ShapeDtypeStruct((SHARD, HEADS * HEAD), jnp.bfloat16),
            jax.ShapeDtypeStruct((TOK, MODEL), jnp.bfloat16),
        ),
        in_specs=[pl.BlockSpec(memory_space=pltpu.SMEM), vmem, vmem, any_space],
        out_specs=(vmem, any_space),
        scratch_shapes=[
            pltpu.VMEM((HEAD, 3 * SHARD), jnp.bfloat16),
            pltpu.VMEM((8, BQ), jnp.float32),
            pltpu.VMEM((8, BQ), jnp.float32),
            pltpu.VMEM((HEADS, HEAD, BQ), jnp.float32),
            pltpu.SemaphoreType.DMA,
        ],
        compiler_params=pltpu.CompilerParams(vmem_limit_bytes=VMEM_LIMIT),
        name="attention",
    )(doc_lengths, queries, kv, hidden)


def per_device(
    residual, shared_out, expert_out, expert_id, gate_value, doc_lengths, norm_gain, w_query,
    key_value_weight, query_gain, key_gain,
):
    hidden, queries, kv = exchange(
        residual,
        shared_out,
        expert_out.reshape(N_EXP, SLOTS, MODEL),
        expert_id,
        gate_value,
        norm_gain.reshape(1, MODEL),
        w_query,
        key_value_weight,
        query_gain.reshape(1, HEAD),
        key_gain.reshape(1, HEAD),
    )
    attended, hidden_out = attention(
        doc_lengths, queries.reshape(SHARD, HEADS * HEAD), kv.reshape(3, 2, SHARD, HEAD), hidden
    )
    return (hidden_out, attended)


def solution(mesh):
    placed = (
        P(("ctx", "exp"), None),
        P(("ctx", "exp"), None),
        P("ctx", "exp", None, None, None, None),
        P(("ctx", "exp"), None),
        P(("ctx", "exp"), None),
        P(),
        P(),
        P("ctx", "exp"),
        P("ctx", None),
        P(),
        P(),
    )
    return jax.shard_map(
        per_device,
        mesh=mesh,
        in_specs=placed,
        out_specs=(P(("ctx", "exp"), None), P("ctx", "exp")),
        check_vma=False,
    )
```

time: 309 us -> 189 us (0.61)
  Pallas kernels: 0 us -> 181 us
  waiting for transfers between devices: 149 us -> 0 us
  matrix products: 71 us -> 0 us
  other arithmetic: 41.2 us -> 0 us
  between operations: 16.1 us -> 0.64 us
  local copies, waits for them, and re-layouts: 19.1 us -> 4.15 us
  starting transfers between devices: 11 us -> 0 us
    pallas_call x0 -> x2, Pallas kernels: none -> 181 us  [the longest x1 128 us: exchange(): pl.pallas_call(exchange_kernel, out_shape=(jax.ShapeDtypeStruct((TOK, MOD...]
    all_gather x3 -> x0, waiting for transfers between devices: 110 us -> none  [the longest x1 71.5 us: per_device(): shard_rows = lax.all_gather(normed, 'exp', axis=0, tiled=True)]
    dot_general x8 -> x0, matrix products: 71 us -> none  [the longest x3 32.8 us: update(): jnp.einsum('hqk,kd->hqd', probs, kv_block[:, HEAD_DIM:], preferred_elemen...]
    all_to_all x1 -> x0, waiting for transfers between devices: 38.6 us -> none  [per_device(): lax.all_to_all(held_rows, 'exp', split_axis=0, concat_axis=0, tiled=True)]
    reduce_sum x8 -> x0, other arithmetic: 22.7 us -> none  [the longest x3 17.1 us: update(): run_sum = run_sum * factor + jnp.sum(weights_now, axis=2)]
    convert_element_type x4 -> x0, other arithmetic: 6.41 us -> none  [the longest x1 3.23 us: per_device(): normed = rms_scale(summed, norm_gain).astype(jnp.bfloat16)]
    and x1 -> x0, other arithmetic: 6.21 us -> none  [absorb(): (key_doc[None, :] == query_doc[:, None]) & (key_pos[None, :] <= query_pos...]
    ppermute x2 -> x0, starting transfers between devices: 5.56 us -> none  [from_behind(): lax.ppermute(value, axis, [(source, source + steps) for source in range(i...]
  transfers between devices with their start and end apart: 6 -> 0, of which waited for: 4 -> 0; matrix products, arithmetic and copies ran while one was open for 29% -> 0% of each run, Pallas kernels for 0% -> 0%
where the time goes in v1:
time: 189 us; the launch traced here: 186 us
  Pallas kernels  181 us (96%)
  local copies, waits for them, and re-layouts  4.15 us (2%)
    pallas_call x1, Pallas kernels, exchange(): pl.pallas_call(exchange_kernel, out_shape=(jax.ShapeDtypeStruct((TOK, MOD...  128 us
    pallas_call x1, Pallas kernels, attention(): pl.pallas_call(attention_kernel, out_shape=(jax.ShapeDtypeStruct((SHARD,...  53.6 us

profile of v1, /device:TPU:65, one launch (start us, length us, event | category | flops | bytes accessed | tf_op | source)
XLA Modules:
  0.0 185.9 jit_solution(11849297189808025377)
XLA Ops:
  0.6 1.4 reshape.23.gain_ref
  2.0 1.4 copy.13.eid_ref
  3.4 1.4 copy.14.gate_ref
  4.8 127.5 %exchange.1 = (bf16[128,6400]{1,0:T(8,128)(2,1)}, bf16[8,4,32,640]{3,2,1,0:T(8,128)(2,1)}, bf16[3,2,8,4,32,128]{5,4,3,2,1,0:T(8,128)(2,1)}) custom-call(bf16[128,6400]{1,0:T(8,128)(2,1)} %res_hbm.1, bf16[128,6400]{1,0:T(8,128)(2,1)} %sh_hbm.1, bf16[8,32,6400]{2,1,0:T(8,128)(2,1)} %bitcast.7, s32[128,1]{1,0:T(8,128)} %copy.13.eid_ref, ...), custom_call_target="tpu_custom_call" | custom-call | flops 10066329600 | bytes 16777216 | tf_op jit(solution)/shard_map/exchange/pallas_call | solution.py:243
  132.3 53.6 %attention.1 = (bf16[1024,640]{1,0:T(8,128)(2,1)}, bf16[128,6400]{1,0:T(8,128)(2,1)}) custom-call(s32[32]{0:T(128)} %doc_ref.1, bf16[1024,640]{1,0:T(8,128)(2,1)} %bitcast.6, bf16[3,2,1024,128]{3,2,1,0:T(8,128)(2,1)} %bitcast.5, bf16[128,6400]{1,0:T(8,128)(2,1)} %get-tuple-element.9.hid_hbm), custom_call_target="tpu_custom_call" | custom-call | tf_op jit(solution)/shard_map/attention/pallas_call | solution.py:366

commit v2 on v1

--- a/solution.py
+++ b/solution.py
@@ -22,6 +22,7 @@
 FW = MODEL // FCH
 PCH = 4
 PR = TOK // PCH
+PH = PR // 2
 PM = N_EXP * PR
 WROWS = 400
 WA = 208
@@ -39,7 +40,7 @@
     res_hbm, sh_hbm, ex_hbm, eid_ref, gate_ref, gain_ref, wq_hbm, wkv_hbm, qg_ref, kg_ref,
     hid_hbm, q_hbm, kv_hbm,
     slots, res, sh, summed, hid, xall, wall, qbuf, kvbuf,
-    loc_sem, a_send, a_recv, a_own, w_send, w_recv1, w_recv2, x_send, x_recv, s_send, s_recv,
+    loc_sem, a_send, a_recv, a_own, w_send, w_recv1, w_recv2, x_send, x_recv, f_send, f_recv, s_send, s_recv,
     h_send, h_recv, hs_send, hs_recv, out_sem,
 ):
     c = lax.axis_index("ctx")
@@ -121,21 +122,20 @@
 
     experts = 2 * N_EXP
     chosen = eid_ref[...]
-    named = chosen == lax.broadcasted_iota(jnp.int32, (TOK, experts), 1)
-    named = jnp.where(named, 1.0, 0.0)
-    earlier = lax.broadcasted_iota(jnp.int32, (TOK, TOK), 1) < lax.broadcasted_iota(
-        jnp.int32, (TOK, TOK), 0
+    named = jnp.where(chosen == lax.broadcasted_iota(jnp.int32, (experts, TOK), 0), 1.0, 0.0)
+    earlier = lax.broadcasted_iota(jnp.int32, (TOK, TOK), 0) < lax.broadcasted_iota(
+        jnp.int32, (TOK, TOK), 1
     )
     before = jnp.dot(
+        named.astype(jnp.bfloat16),
         jnp.where(earlier, 1.0, 0.0).astype(jnp.bfloat16),
-        named.astype(jnp.bfloat16),
         preferred_element_type=jnp.float32,
     )
-    slot = jnp.sum(named * before, axis=1, keepdims=True)
+    slot = jnp.sum(named * before, axis=0, keepdims=True)
     row = chosen.astype(jnp.float32) * float(SLOTS // 2) + slot
-    lane = lax.broadcasted_iota(jnp.int32, (TOK, N_EXP * SLOTS), 1).astype(jnp.float32)
-    pick = jnp.where(lane == row, 1.0, 0.0).astype(jnp.bfloat16)
-    gate = gate_ref[...]
+    place = lax.broadcasted_iota(jnp.int32, (N_EXP * SLOTS, TOK), 0).astype(jnp.float32)
+    pick = jnp.where(place == row, 1.0, 0.0).T.astype(jnp.bfloat16)
+    gate = jnp.broadcast_to(gate_ref[...], (TOK, TOK)).T[:, :1]
 
     for d in (1, 3, 2):
         done(half_a(0), w_recv1.at[0, d])
@@ -163,16 +163,29 @@
         squares = squares + jnp.sum(total * total, axis=1, keepdims=True)
     scale = lax.rsqrt(squares * (1.0 / MODEL) + EPS)
     here = pl.ds(pl.multiple_of(e * PR, PR), PR)
-    gain = gain_ref[...]
+    gain = gain_ref[...][None, :]
     for p in range(PCH):
         rows = slice(p * PR, (p + 1) * PR)
         xall[p, here, :] = (summed[rows, :] * scale[rows] * gain).astype(jnp.bfloat16)
         block = xall.at[p, here, :]
-        for d in (1, 3, 2):
-            remote(block, block, x_send, x_recv.at[p, d], along_y(d))
+        remote(block, block, x_send, x_recv.at[p, 0], along_y(1))
+        remote(block, block, x_send, x_recv.at[p, 1], along_y(3))
         remote(block, block, s_send, s_recv.at[p], sibling)
     store_hid = pltpu.make_async_copy(hid, hid_hbm, out_sem.at[0])
     store_hid.start()
+
+    def rows_of(p, d, start, count):
+        source = ((y + d + 4) % 4) * 2 + k
+        return xall.at[p, pl.ds(pl.multiple_of(source * PR + start, 16), count), :]
+
+    @pl.loop(0, PCH)
+    def _(p):
+        for side, d in ((0, -1), (1, 1)):
+            block = rows_of(p, d, 0, PR)
+            done(block, x_recv.at[p, side])
+            part = rows_of(p, d, side * PH, PH)
+            remote(part, part, f_send, f_recv.at[p, side], along_y(-d))
+            remote(block, block, s_send, s_recv.at[p], sibling)
 
     done(wall.at[pl.ds(0, 12 * WA), :], w_recv2.at[0])
     done(wall.at[pl.ds(0, 12 * WB), :], w_recv2.at[1])
@@ -185,11 +198,10 @@
 
     @pl.loop(0, PCH)
     def _(p):
-        for d in (1, 3, 2):
-            source = ((y - d + 4) % 4) * 2 + k
-            block = xall.at[p, pl.ds(pl.multiple_of(source * PR, PR), PR), :]
-            done(block, x_recv.at[p, d])
-            remote(block, block, s_send, s_recv.at[p], sibling)
+        for side in range(2):
+            part = rows_of(p, 2, side * PH, PH)
+            done(part, f_recv.at[p, side])
+            remote(part, part, s_send, s_recv.at[p], sibling)
         done(xall.at[p, pl.ds(0, 4 * PR), :], s_recv.at[p])
 
         last = jnp.dot(
@@ -198,7 +210,7 @@
         raw = last[:, HEAD:]
         part = jnp.where(k == 0, rms_rows(raw, kg_ref[...]), raw).astype(jnp.bfloat16)
         kvbuf[p] = part.reshape(N_EXP, PR, HEAD)
-        for dist in (1, 2):
+        for dist in (2, 1):
             remote(
                 kvbuf.at[p], kv_hbm.at[2 - dist, k, :, p], h_send, h_recv.at[p, dist], along_ctx(dist)
             )
@@ -225,7 +237,8 @@
     done(ex_hbm.at[pl.ds(0, N_EXP - 1)], a_send)
     done(wall.at[pl.ds(0, 15 * WA), :], w_send.at[0])
     done(wall.at[pl.ds(0, 15 * WB), :], w_send.at[1])
-    done(xall.at[:, pl.ds(0, 3 * PR), :], x_send)
+    done(xall.at[:, pl.ds(0, 2 * PR), :], x_send)
+    done(xall.at[:, pl.ds(0, PR), :], f_send)
     done(xall.at[:, pl.ds(0, 4 * PR), :], s_send)
     done(kv_hbm.at[pl.ds(0, 2), 0], h_send)
     done(kv_hbm.at[:, 0], hs_send)
@@ -267,7 +280,9 @@
             dma((2, 4)),
             dma((2,)),
             dma,
-            dma((PCH, 4)),
+            dma((PCH, 2)),
+            dma,
+            dma((PCH, 2)),
             dma,
             dma((PCH,)),
             dma,
@@ -286,97 +301,131 @@
     )(residual, shared_out, expert_rows, expert_id, gate, gain, w_query, w_kv, q_gain, k_gain)
 
 
-BQ = 256
-BK = 256
+BQ = 512
+BK = 512
 NEG = -1e30
-LOG2E = math.log2(math.e)
+FACTOR = HEAD ** (-0.5) * math.log2(math.e)
 
 
 def attention_kernel(
-    doc_ref, q_ref, kv_ref, hid_hbm, out_ref, hid_out_hbm, vt, m_ref, l_ref, acc_ref, sem
+    doc_ref, q_ref, kv_ref, hid_hbm, out_ref, hid_out_hbm, values_t, queries_t, s_ref, m_ref, l_ref,
+    acc_ref, hid, sem,
 ):
     c = lax.axis_index("ctx")
-    copy = pltpu.make_async_copy(hid_hbm, hid_out_hbm, sem)
-    copy.start()
-    window = c * SHARD - 2 * SHARD
-    span = 3 * SHARD
-    for part in range(3):
-        vt[:, part * SHARD : (part + 1) * SHARD] = kv_ref[part, 1].T
-
-    factor = HEAD ** (-0.5) * LOG2E
-
-    @pl.loop(0, SHARD // BQ)
-    def _(qb):
-        q_low = 2 * SHARD + qb * BQ
-        q_rows = pl.ds(pl.multiple_of(qb * BQ, BQ), BQ)
-        position = q_low + lax.broadcasted_iota(jnp.int32, (1, BQ), 1)
-
-        def starts(i, carried):
-            end, first, least = carried
-            end = end + doc_ref[i]
-            first = jnp.where(end <= position, end, first)
-            return end, first, jnp.where(end <= q_low, end, least)
-
-        _, first, least = lax.fori_loop(
-            0, doc_ref.shape[0], starts,
-            (0 - window, jnp.zeros((1, BQ), jnp.int32) - window, 0 - window),
-        )
-        m_ref[...] = jnp.full(m_ref.shape, NEG, jnp.float32)
-        l_ref[...] = jnp.zeros(l_ref.shape, jnp.float32)
-        acc_ref[...] = jnp.zeros(acc_ref.shape, jnp.float32)
-
-        def block(kb, carried):
-            k_low = pl.multiple_of(kb * BK, BK)
-            keys = kv_ref.at[kb // (SHARD // BK), 0][
-                pl.ds(pl.multiple_of((kb % (SHARD // BK)) * BK, BK), BK), :
-            ]
-            values = vt[:, pl.ds(k_low, BK)]
-            k_position = k_low + lax.broadcasted_iota(jnp.int32, (BK, 1), 0)
+    qb = pl.program_id(0)
+    steps = SHARD // BQ
+    per = SHARD // BK
+    load_hid = pltpu.make_async_copy(hid_hbm, hid, sem.at[0])
+    store_hid = pltpu.make_async_copy(hid, hid_out_hbm, sem.at[1])
+
+    @pl.when(qb == 0)
+    def _():
+        load_hid.start()
+        for part in range(3):
+            values_t[:, part * SHARD : (part + 1) * SHARD] = kv_ref[part, 1].T
+
+    queries_t[...] = q_ref[...].T
+
+    window = (c - 2) * SHARD
+    q_low = 2 * SHARD + qb * BQ
+    position = q_low + lax.broadcasted_iota(jnp.int32, (1, BQ), 1)
+
+    def starts(i, carried):
+        end, first, least, most = carried
+        end = end + doc_ref[i]
+        first = jnp.where(end <= position, end, first)
+        least = jnp.where(end <= q_low, end, least)
+        most = jnp.where(end <= q_low + BQ - 1, end, most)
+        return end, first, least, most
+
+    _, first, least, most = lax.fori_loop(
+        0, doc_ref.shape[0], starts,
+        (0 - window, jnp.zeros((1, BQ), jnp.int32) - window, 0 - window, 0 - window),
+    )
+    low, high = least // BK, (q_low + BQ) // BK
+    m_ref[...] = jnp.full(m_ref.shape, NEG, jnp.float32)
+
+    def score(kb, masked):
+        k_low = pl.multiple_of(kb * BK, BK)
+        keys = kv_ref.at[kb // per, 0][pl.ds(pl.multiple_of((kb % per) * BK, BK), BK), :]
+        if masked:
+            k_position = k_low + lax.broadcasted_iota(jnp.int32, (BK, BQ), 0)
             allowed = (k_position >= first) & (k_position <= position)
-            for h in range(HEADS):
-                scores = lax.dot_general(
-                    keys, q_ref[q_rows, h * HEAD : (h + 1) * HEAD], (((1,), (1,)), ((), ())),
-                    preferred_element_type=jnp.float32,
-                )
-                scores = jnp.where(allowed, scores * factor, NEG)
-                old = m_ref[h : h + 1, :]
-                new = jnp.maximum(old, jnp.max(scores, axis=0, keepdims=True))
-                weights = jnp.where(allowed, jnp.exp2(scores - new), 0.0)
-                shrink = jnp.exp2(old - new)
-                m_ref[h : h + 1, :] = new
-                l_ref[h : h + 1, :] = l_ref[h : h + 1, :] * shrink + jnp.sum(
-                    weights, axis=0, keepdims=True
-                )
-                acc_ref[h] = acc_ref[h] * shrink + jnp.dot(
-                    values, weights.astype(jnp.bfloat16), preferred_element_type=jnp.float32
-                )
-            return carried
-
-        lax.fori_loop(least // BK, (q_low + BQ) // BK, block, 0)
         for h in range(HEADS):
-            finished = acc_ref[h] / l_ref[h : h + 1, :]
-            out_ref[q_rows, h * HEAD : (h + 1) * HEAD] = finished.T.astype(jnp.bfloat16)
-
-    copy.wait()
+            scores = jnp.dot(
+                keys, queries_t[h * HEAD : (h + 1) * HEAD, :], preferred_element_type=jnp.float32
+            )
+            if masked:
+                scores = jnp.where(allowed, scores, NEG)
+            s_ref[h, pl.ds(k_low, BK), :] = scores
+            m_ref[h] = jnp.maximum(m_ref[h], jnp.max(scores.reshape(BK // 8, 8, BQ), axis=0))
+
+    @pl.loop(low, high)
+    def _(kb):
+        edge = (kb * BK < most) | (kb * BK + BK > q_low + 1)
+        pl.when(edge)(lambda: score(kb, True))
+        pl.when(jnp.logical_not(edge))(lambda: score(kb, False))
+
+    for h in range(HEADS):
+        largest = jnp.max(m_ref[h], axis=0, keepdims=True) * FACTOR
+        m_ref[h] = jnp.broadcast_to(largest, (8, BQ))
+    l_ref[...] = jnp.zeros(l_ref.shape, jnp.float32)
+    acc_ref[...] = jnp.zeros(acc_ref.shape, jnp.float32)
+
+    @pl.loop(low, high)
+    def _(kb):
+        k_low = pl.multiple_of(kb * BK, BK)
+        values = values_t[:, pl.ds(k_low, BK)]
+        for h in range(HEADS):
+            scores = s_ref[h, pl.ds(k_low, BK), :].reshape(BK // 8, 8, BQ)
+            weights = jnp.exp2(scores * FACTOR - m_ref[h][None])
+            l_ref[h] += jnp.sum(weights, axis=0)
+            acc_ref[h] += jnp.dot(
+                values, weights.reshape(BK, BQ).astype(jnp.bfloat16),
+                preferred_element_type=jnp.float32,
+            )
+
+    for h in range(HEADS):
+        total = jnp.sum(l_ref[h], axis=0, keepdims=True)
+        out_ref[:, h * HEAD : (h + 1) * HEAD] = (acc_ref[h] / total).T.astype(jnp.bfloat16)
+
+    @pl.when(qb == 0)
+    def _():
+        load_hid.wait()
+        store_hid.start()
+
+    @pl.when(qb == steps - 1)
+    def _():
+        store_hid.wait()
 
 
 def attention(doc_lengths, queries, kv, hidden):
-    vmem = pl.BlockSpec(memory_space=pltpu.VMEM)
     any_space = pl.BlockSpec(memory_space=pl.ANY)
+    vmem = pltpu.VMEM
+    f32, bf16 = jnp.float32, jnp.bfloat16
     return pl.pallas_call(
         attention_kernel,
+        grid=(SHARD // BQ,),
         out_shape=(
-            jax.ShapeDtypeStruct((SHARD, HEADS * HEAD), jnp.bfloat16),
-            jax.ShapeDtypeStruct((TOK, MODEL), jnp.bfloat16),
+            jax.ShapeDtypeStruct((SHARD, HEADS * HEAD), bf16),
+            jax.ShapeDtypeStruct((TOK, MODEL), bf16),
         ),
-        in_specs=[pl.BlockSpec(memory_space=pltpu.SMEM), vmem, vmem, any_space],
-        out_specs=(vmem, any_space),
+        in_specs=[
+            pl.BlockSpec(memory_space=pltpu.SMEM),
+            pl.BlockSpec((BQ, HEADS * HEAD), lambda i: (i, 0)),
+            pl.BlockSpec((3, 2, SHARD, HEAD), lambda i: (0, 0, 0, 0)),
+            any_space,
+        ],
+        out_specs=(pl.BlockSpec((BQ, HEADS * HEAD), lambda i: (i, 0)), any_space),
         scratch_shapes=[
-            pltpu.VMEM((HEAD, 3 * SHARD), jnp.bfloat16),
-            pltpu.VMEM((8, BQ), jnp.float32),
-            pltpu.VMEM((8, BQ), jnp.float32),
-            pltpu.VMEM((HEADS, HEAD, BQ), jnp.float32),
-            pltpu.SemaphoreType.DMA,
+            vmem((HEAD, 3 * SHARD), bf16),
+            vmem((HEADS * HEAD, BQ), bf16),
+            vmem((HEADS, 3 * SHARD, BQ), f32),
+            vmem((HEADS, 8, BQ), f32),
+            vmem((HEADS, 8, BQ), f32),
+            vmem((HEADS, HEAD, BQ), f32),
+            vmem((TOK, MODEL), bf16),
+            pltpu.SemaphoreType.DMA((2,)),
         ],
         compiler_params=pltpu.CompilerParams(vmem_limit_bytes=VMEM_LIMIT),
         name="attention",
@@ -391,9 +440,9 @@
         residual,
         shared_out,
         expert_out.reshape(N_EXP, SLOTS, MODEL),
-        expert_id,
-        gate_value,
-        norm_gain.reshape(1, MODEL),
+        expert_id.reshape(1, TOK),
+        gate_value.reshape(1, TOK),
+        norm_gain,
         w_query,
         key_value_weight,
         query_gain.reshape(1, HEAD),

time: 189 us -> 132 us (0.70)
  the two profiles are of different devices: /device:TPU:65 before, /device:TPU:7 now
where the time goes in v2:
time: 132 us; the launch traced here: 131 us
  Pallas kernels  131 us (99%)
    pallas_call x1, Pallas kernels, exchange(): pl.pallas_call(exchange_kernel, out_shape=(jax.ShapeDtypeStruct((TOK, MOD...  112 us
    pallas_call x1, Pallas kernels, attention(): pl.pallas_call(attention_kernel, grid=(SHARD // BQ,), out_shape=(jax.Shap...  18.6 us

profile of v2, /device:TPU:7, one launch (start us, length us, event | category | flops | bytes accessed | tf_op | source)
XLA Modules:
  0.0 131.3 jit_solution(16406757716718427776)
XLA Ops:
  0.6 112.1 %exchange.1 = (bf16[128,6400]{1,0:T(8,128)(2,1)}, bf16[8,4,32,640]{3,2,1,0:T(8,128)(2,1)}, bf16[3,2,8,4,32,128]{5,4,3,2,1,0:T(8,128)(2,1)}) custom-call(bf16[128,6400]{1,0:T(8,128)(2,1)} %res_hbm.1, bf16[128,6400]{1,0:T(8,128)(2,1)} %sh_hbm.1, bf16[8,32,6400]{2,1,0:T(8,128)(2,1)} %bitcast.9, s32[1,128]{1,0:T(1,128)} %bitcast.10, f32[1,128]{1,0:T(1,128)} %bitcast.11, ...), custom_call_target="tpu_custom_call" | custom-call | flops 10066329600 | bytes 16777216 | tf_op jit(solution)/shard_map/exchange/pallas_call | solution.py:256
  112.8 18.6 %attention.1 = (bf16[1024,640]{1,0:T(8,128)(2,1)}, bf16[128,6400]{1,0:T(8,128)(2,1)}) custom-call(s32[32]{0:T(128)} %doc_ref.1, bf16[1024,640]{1,0:T(8,128)(2,1)} %bitcast.8, bf16[3,2,1024,128]{3,2,1,0:T(8,128)(2,1)} %bitcast.7, bf16[128,6400]{1,0:T(8,128)(2,1)} %get-tuple-element.9.hid_hbm), custom_call_target="tpu_custom_call" | custom-call | tf_op jit(solution)/shard_map/attention/pallas_call | solution.py:406

commit v3 on v2

--- a/solution.py
+++ b/solution.py
@@ -20,9 +20,9 @@
 SLOTS = 32
 FCH = 5
 FW = MODEL // FCH
-PCH = 4
+PCH = 8
 PR = TOK // PCH
-PH = PR // 2
+AHEAD = 3
 PM = N_EXP * PR
 WROWS = 400
 WA = 208
@@ -164,44 +164,60 @@
     scale = lax.rsqrt(squares * (1.0 / MODEL) + EPS)
     here = pl.ds(pl.multiple_of(e * PR, PR), PR)
     gain = gain_ref[...][None, :]
+    def rows_of(p, d):
+        source = ((y + d + 4) % 4) * 2 + k
+        return xall.at[p, pl.ds(pl.multiple_of(source * PR, PR), PR), :]
+
+    def send_chunk(p):
+        block = rows_of(p, 0)
+        remote(block, block, x_send, x_recv.at[p, 0], along_y(1))
+        remote(block, block, x_send, x_recv.at[p, 1], along_y(3))
+        remote(block, block, s_send, s_recv.at[p], sibling)
+
     for p in range(PCH):
         rows = slice(p * PR, (p + 1) * PR)
         xall[p, here, :] = (summed[rows, :] * scale[rows] * gain).astype(jnp.bfloat16)
-        block = xall.at[p, here, :]
-        remote(block, block, x_send, x_recv.at[p, 0], along_y(1))
-        remote(block, block, x_send, x_recv.at[p, 1], along_y(3))
-        remote(block, block, s_send, s_recv.at[p], sibling)
+        if p < AHEAD:
+            send_chunk(p)
     store_hid = pltpu.make_async_copy(hid, hid_hbm, out_sem.at[0])
     store_hid.start()
 
-    def rows_of(p, d, start, count):
-        source = ((y + d + 4) % 4) * 2 + k
-        return xall.at[p, pl.ds(pl.multiple_of(source * PR + start, 16), count), :]
+    def pass_on(p):
+        up = 1 - 2 * (p % 2)
+        done(rows_of(p, -1), x_recv.at[p, 0])
+        done(rows_of(p, 1), x_recv.at[p, 1])
+        part = rows_of(p, -up)
+        remote(part, part, f_send, f_recv.at[p], along_y(up))
+        for d in (-1, 1):
+            block = rows_of(p, d)
+            remote(block, block, s_send, s_recv.at[p], sibling)
+
+        @pl.when(p < PCH - AHEAD)
+        def _():
+            send_chunk(p + AHEAD)
+
+    @pl.loop(0, PCH // 2)
+    def _(p):
+        pass_on(p)
+
+    done(wall.at[pl.ds(0, 12 * WA), :], w_recv2.at[0])
+    done(wall.at[pl.ds(0, 12 * WB), :], w_recv2.at[1])
+
+    def pass_halo(p):
+        for dist in (1, 2):
+            part = kv_hbm.at[k, 2 - dist, :, p]
+            done(part, h_recv.at[p, dist])
+            remote(part, part, hs_send, hs_recv, sibling)
 
     @pl.loop(0, PCH)
     def _(p):
-        for side, d in ((0, -1), (1, 1)):
-            block = rows_of(p, d, 0, PR)
-            done(block, x_recv.at[p, side])
-            part = rows_of(p, d, side * PH, PH)
-            remote(part, part, f_send, f_recv.at[p, side], along_y(-d))
-            remote(block, block, s_send, s_recv.at[p], sibling)
-
-    done(wall.at[pl.ds(0, 12 * WA), :], w_recv2.at[0])
-    done(wall.at[pl.ds(0, 12 * WB), :], w_recv2.at[1])
-
-    def pass_halo(p):
-        for dist in (1, 2):
-            part = kv_hbm.at[2 - dist, k, :, p]
-            done(part, h_recv.at[p, dist])
-            remote(part, part, hs_send, hs_recv, sibling)
-
-    @pl.loop(0, PCH)
-    def _(p):
-        for side in range(2):
-            part = rows_of(p, 2, side * PH, PH)
-            done(part, f_recv.at[p, side])
-            remote(part, part, s_send, s_recv.at[p], sibling)
+        @pl.when((p >= PCH // 2 - 2) & (p < PCH - 2))
+        def _():
+            pass_on(p + 2)
+
+        part = rows_of(p, 2)
+        done(part, f_recv.at[p])
+        remote(part, part, s_send, s_recv.at[p], sibling)
         done(xall.at[p, pl.ds(0, 4 * PR), :], s_recv.at[p])
 
         last = jnp.dot(
@@ -212,10 +228,10 @@
         kvbuf[p] = part.reshape(N_EXP, PR, HEAD)
         for dist in (2, 1):
             remote(
-                kvbuf.at[p], kv_hbm.at[2 - dist, k, :, p], h_send, h_recv.at[p, dist], along_ctx(dist)
+                kvbuf.at[p], kv_hbm.at[k, 2 - dist, :, p], h_send, h_recv.at[p, dist], along_ctx(dist)
             )
-        remote(kvbuf.at[p], kv_hbm.at[2, k, :, p], hs_send, hs_recv, sibling)
-        pltpu.make_async_copy(kvbuf.at[p], kv_hbm.at[2, k, :, p], out_sem.at[1]).start()
+        remote(kvbuf.at[p], kv_hbm.at[k, 2, :, p], hs_send, hs_recv, sibling)
+        pltpu.make_async_copy(kvbuf.at[p], kv_hbm.at[k, 2, :, p], out_sem.at[1]).start()
         head = rms_rows(last[:, :HEAD], qg_ref[...]).astype(jnp.bfloat16)
         qbuf[p, :, :, (HEADS - 1) * HEAD :] = head.reshape(N_EXP, PR, HEAD)
         for pair in range((HEADS - 1) // 2):
@@ -240,9 +256,9 @@
     done(xall.at[:, pl.ds(0, 2 * PR), :], x_send)
     done(xall.at[:, pl.ds(0, PR), :], f_send)
     done(xall.at[:, pl.ds(0, 4 * PR), :], s_send)
-    done(kv_hbm.at[pl.ds(0, 2), 0], h_send)
-    done(kv_hbm.at[:, 0], hs_send)
-    done(kv_hbm.at[:, 0], hs_recv)
+    done(kv_hbm.at[0, pl.ds(0, 2)], h_send)
+    done(kv_hbm.at[0], hs_send)
+    done(kv_hbm.at[0], hs_recv)
     store_hid.wait()
     done(kv_hbm.at[0, 0], out_sem.at[1])
     done(q_hbm, out_sem.at[2])
@@ -258,7 +274,7 @@
         out_shape=(
             jax.ShapeDtypeStruct((TOK, MODEL), bf16),
             jax.ShapeDtypeStruct((N_EXP, PCH, PR, HEADS * HEAD), bf16),
-            jax.ShapeDtypeStruct((3, 2, N_EXP, PCH, PR, HEAD), bf16),
+            jax.ShapeDtypeStruct((2, 3, N_EXP, PCH, PR, HEAD), bf16),
         ),
         in_specs=[any_space] * 3 + [vmem] * 3 + [any_space] * 2 + [vmem] * 2,
         out_specs=(any_space, any_space, any_space),
@@ -282,7 +298,7 @@
             dma,
             dma((PCH, 2)),
             dma,
-            dma((PCH, 2)),
+            dma((PCH,)),
             dma,
             dma((PCH,)),
             dma,
@@ -314,20 +330,18 @@
     c = lax.axis_index("ctx")
     qb = pl.program_id(0)
     steps = SHARD // BQ
-    per = SHARD // BK
     load_hid = pltpu.make_async_copy(hid_hbm, hid, sem.at[0])
     store_hid = pltpu.make_async_copy(hid, hid_out_hbm, sem.at[1])
 
     @pl.when(qb == 0)
     def _():
         load_hid.start()
-        for part in range(3):
-            values_t[:, part * SHARD : (part + 1) * SHARD] = kv_ref[part, 1].T
+        values_t[...] = kv_ref[1].T
 
     queries_t[...] = q_ref[...].T
 
     window = (c - 2) * SHARD
-    q_low = 2 * SHARD + qb * BQ
+    q_low = pl.multiple_of(2 * SHARD + qb * BQ, BQ)
     position = q_low + lax.broadcasted_iota(jnp.int32, (1, BQ), 1)
 
     def starts(i, carried):
@@ -342,29 +356,57 @@
         0, doc_ref.shape[0], starts,
         (0 - window, jnp.zeros((1, BQ), jnp.int32) - window, 0 - window, 0 - window),
     )
-    low, high = least // BK, (q_low + BQ) // BK
     m_ref[...] = jnp.full(m_ref.shape, NEG, jnp.float32)
 
-    def score(kb, masked):
-        k_low = pl.multiple_of(kb * BK, BK)
-        keys = kv_ref.at[kb // per, 0][pl.ds(pl.multiple_of((kb % per) * BK, BK), BK), :]
+    def score(k_low, count, skip, masked):
+        keys = kv_ref[0, pl.ds(k_low, count), :]
         if masked:
-            k_position = k_low + lax.broadcasted_iota(jnp.int32, (BK, BQ), 0)
-            allowed = (k_position >= first) & (k_position <= position)
+            k_position = k_low + lax.broadcasted_iota(jnp.int32, (count, BQ - skip), 0)
+            allowed = (k_position >= first[:, skip:]) & (k_position <= position[:, skip:])
         for h in range(HEADS):
             scores = jnp.dot(
-                keys, queries_t[h * HEAD : (h + 1) * HEAD, :], preferred_element_type=jnp.float32
+                keys, queries_t[h * HEAD : (h + 1) * HEAD, skip:],
+                preferred_element_type=jnp.float32,
             )
             if masked:
                 scores = jnp.where(allowed, scores, NEG)
-            s_ref[h, pl.ds(k_low, BK), :] = scores
-            m_ref[h] = jnp.maximum(m_ref[h], jnp.max(scores.reshape(BK // 8, 8, BQ), axis=0))
-
-    @pl.loop(low, high)
-    def _(kb):
-        edge = (kb * BK < most) | (kb * BK + BK > q_low + 1)
-        pl.when(edge)(lambda: score(kb, True))
-        pl.when(jnp.logical_not(edge))(lambda: score(kb, False))
+            s_ref[h, pl.ds(k_low, count), skip:] = scores
+            m_ref[h, :, skip:] = jnp.maximum(
+                m_ref[h, :, skip:], jnp.max(scores.reshape(count // 8, 8, BQ - skip), axis=0)
+            )
+
+    def weigh(k_low, count, skip):
+        values = values_t[:, pl.ds(k_low, count)]
+        for h in range(HEADS):
+            scores = s_ref[h, pl.ds(k_low, count), skip:].reshape(count // 8, 8, BQ - skip)
+            weights = jnp.exp2(scores * FACTOR - m_ref[h, :, skip:][None])
+            l_ref[h, :, skip:] += jnp.sum(weights, axis=0)
+            acc_ref[h, :, skip:] += jnp.dot(
+                values, weights.reshape(count, BQ - skip).astype(jnp.bfloat16),
+                preferred_element_type=jnp.float32,
+            )
+
+    half = BK // 2
+    low = jnp.minimum(least // half, q_low // half)
+    odd = (q_low // half - low) % 2
+    whole = (q_low - (low + odd) * half) // BK
+
+    def each_block(act):
+        @pl.when(odd == 1)
+        def _():
+            act(pl.multiple_of(low * half, half), half)
+
+        @pl.loop(0, whole)
+        def _(i):
+            act(pl.multiple_of((low + odd) * half + i * BK, half), BK)
+
+    def score_block(k_low, count):
+        pl.when(k_low < most)(lambda: score(k_low, count, 0, True))
+        pl.when(k_low >= most)(lambda: score(k_low, count, 0, False))
+
+    each_block(score_block)
+    score(q_low, half, 0, True)
+    score(pl.multiple_of(q_low + half, half), half, half, True)
 
     for h in range(HEADS):
         largest = jnp.max(m_ref[h], axis=0, keepdims=True) * FACTOR
@@ -372,18 +414,9 @@
     l_ref[...] = jnp.zeros(l_ref.shape, jnp.float32)
     acc_ref[...] = jnp.zeros(acc_ref.shape, jnp.float32)
 
-    @pl.loop(low, high)
-    def _(kb):
-        k_low = pl.multiple_of(kb * BK, BK)
-        values = values_t[:, pl.ds(k_low, BK)]
-        for h in range(HEADS):
-            scores = s_ref[h, pl.ds(k_low, BK), :].reshape(BK // 8, 8, BQ)
-            weights = jnp.exp2(scores * FACTOR - m_ref[h][None])
-            l_ref[h] += jnp.sum(weights, axis=0)
-            acc_ref[h] += jnp.dot(
-                values, weights.reshape(BK, BQ).astype(jnp.bfloat16),
-                preferred_element_type=jnp.float32,
-            )
+    each_block(lambda k_low, count: weigh(k_low, count, 0))
+    weigh(q_low, half, 0)
+    weigh(pl.multiple_of(q_low + half, half), half, half)
 
     for h in range(HEADS):
         total = jnp.sum(l_ref[h], axis=0, keepdims=True)
@@ -413,7 +446,7 @@
         in_specs=[
             pl.BlockSpec(memory_space=pltpu.SMEM),
             pl.BlockSpec((BQ, HEADS * HEAD), lambda i: (i, 0)),
-            pl.BlockSpec((3, 2, SHARD, HEAD), lambda i: (0, 0, 0, 0)),
+            pl.BlockSpec((2, 3 * SHARD, HEAD), lambda i: (0, 0, 0)),
             any_space,
         ],
         out_specs=(pl.BlockSpec((BQ, HEADS * HEAD), lambda i: (i, 0)), any_space),
@@ -449,7 +482,7 @@
         key_gain.reshape(1, HEAD),
     )
     attended, hidden_out = attention(
-        doc_lengths, queries.reshape(SHARD, HEADS * HEAD), kv.reshape(3, 2, SHARD, HEAD), hidden
+        doc_lengths, queries.reshape(SHARD, HEADS * HEAD), kv.reshape(2, 3 * SHARD, HEAD), hidden
     )
     return (hidden_out, attended)
 

time: 132 us -> 131 us (level)
  the two profiles are of different devices: /device:TPU:7 before, /device:TPU:65 now
where the time goes in v3:
time: 131 us
  Pallas kernels  130 us (99%)
    pallas_call x1, Pallas kernels, exchange(): pl.pallas_call(exchange_kernel, out_shape=(jax.ShapeDtypeStruct((TOK, MOD...  110 us
    pallas_call x1, Pallas kernels, attention(): pl.pallas_call(attention_kernel, grid=(SHARD // BQ,), out_shape=(jax.Shap...  20 us

profile of v3, /device:TPU:65, one launch (start us, length us, event | category | flops | bytes accessed | tf_op | source)
XLA Modules:
  0.0 130.6 jit_solution(12949658315813936966)
XLA Ops:
  0.6 110.0 %exchange.1 = (bf16[128,6400]{1,0:T(8,128)(2,1)}, bf16[8,8,16,640]{3,2,1,0:T(8,128)(2,1)}, bf16[2,3,8,8,16,128]{5,4,3,2,1,0:T(8,128)(2,1)}) custom-call(bf16[128,6400]{1,0:T(8,128)(2,1)} %res_hbm.1, bf16[128,6400]{1,0:T(8,128)(2,1)} %sh_hbm.1, bf16[8,32,6400]{2,1,0:T(8,128)(2,1)} %bitcast.9, s32[1,128]{1,0:T(1,128)} %bitcast.10, f32[1,128]{1,0:T(1,128)} %bitcast.11, ...), custom_call_target="tpu_custom_call" | custom-call | flops 10066329600 | bytes 16777216 | tf_op jit(solution)/shard_map/exchange/pallas_call | solution.py:272
  110.6 20.0 %attention.1 = (bf16[1024,640]{1,0:T(8,128)(2,1)}, bf16[128,6400]{1,0:T(8,128)(2,1)}) custom-call(s32[32]{0:T(128)} %doc_ref.1, bf16[1024,640]{1,0:T(8,128)(2,1)} %bitcast.8, bf16[2,3072,128]{2,1,0:T(8,128)(2,1)} %bitcast.7, bf16[128,6400]{1,0:T(8,128)(2,1)} %get-tuple-element.9.hid_hbm), custom_call_target="tpu_custom_call" | custom-call | tf_op jit(solution)/shard_map/attention/pallas_call | solution.py:439

commit v4 on v3

--- a/solution.py
+++ b/solution.py
@@ -182,12 +182,14 @@
     store_hid = pltpu.make_async_copy(hid, hid_hbm, out_sem.at[0])
     store_hid.start()
 
+    def half_of(p, d, side):
+        return rows_of(p, d).at[:, pl.ds(side * (MODEL // 2), MODEL // 2)]
+
     def pass_on(p):
-        up = 1 - 2 * (p % 2)
-        done(rows_of(p, -1), x_recv.at[p, 0])
-        done(rows_of(p, 1), x_recv.at[p, 1])
-        part = rows_of(p, -up)
-        remote(part, part, f_send, f_recv.at[p], along_y(up))
+        for side, d in ((0, -1), (1, 1)):
+            done(rows_of(p, d), x_recv.at[p, side])
+            part = half_of(p, d, side)
+            remote(part, part, f_send, f_recv.at[p, side], along_y(-d))
         for d in (-1, 1):
             block = rows_of(p, d)
             remote(block, block, s_send, s_recv.at[p], sibling)
@@ -215,9 +217,10 @@
         def _():
             pass_on(p + 2)
 
-        part = rows_of(p, 2)
-        done(part, f_recv.at[p])
-        remote(part, part, s_send, s_recv.at[p], sibling)
+        for side in range(2):
+            done(half_of(p, 2, side), f_recv.at[p, side])
+        block = rows_of(p, 2)
+        remote(block, block, s_send, s_recv.at[p], sibling)
         done(xall.at[p, pl.ds(0, 4 * PR), :], s_recv.at[p])
 
         last = jnp.dot(
@@ -298,7 +301,7 @@
             dma,
             dma((PCH, 2)),
             dma,
-            dma((PCH,)),
+            dma((PCH, 2)),
             dma,
             dma((PCH,)),
             dma,
@@ -321,10 +324,12 @@
 BK = 512
 NEG = -1e30
 FACTOR = HEAD ** (-0.5) * math.log2(math.e)
+SPREAD = HEAD * FACTOR * 1.01
+EXPONENT_MOST = 100.0
 
 
 def attention_kernel(
-    doc_ref, q_ref, kv_ref, hid_hbm, out_ref, hid_out_hbm, values_t, queries_t, s_ref, m_ref, l_ref,
+    doc_ref, qg_ref, kg_ref, q_ref, kv_ref, hid_hbm, out_ref, hid_out_hbm, values_t, queries_t, s_ref, m_ref, l_ref,
     acc_ref, hid, sem,
 ):
     c = lax.axis_index("ctx")
@@ -356,67 +361,91 @@
         0, doc_ref.shape[0], starts,
         (0 - window, jnp.zeros((1, BQ), jnp.int32) - window, 0 - window, 0 - window),
     )
-    m_ref[...] = jnp.full(m_ref.shape, NEG, jnp.float32)
+    l_ref[...] = jnp.zeros(l_ref.shape, jnp.float32)
+    acc_ref[...] = jnp.zeros(acc_ref.shape, jnp.float32)
+
+    def allowed_pairs(k_low, count, skip):
+        k_position = k_low + lax.broadcasted_iota(jnp.int32, (count, BQ - skip), 0)
+        return (k_position >= first[:, skip:]) & (k_position <= position[:, skip:])
+
+    def raw_scores(k_low, count, skip, h):
+        return jnp.dot(
+            kv_ref[0, pl.ds(k_low, count), :], queries_t[h * HEAD : (h + 1) * HEAD, skip:],
+            preferred_element_type=jnp.float32,
+        )
+
+    def add(k_low, count, skip, h, weights):
+        l_ref[h, :, skip:] += jnp.sum(weights.reshape(count // 8, 8, BQ - skip), axis=0)
+        return weights.astype(jnp.bfloat16)
+
+    def mix(k_low, count, skip, h, probs):
+        acc_ref[h, :, skip:] += jnp.dot(
+            values_t[:, pl.ds(k_low, count)], probs, preferred_element_type=jnp.float32
+        )
+
+    def direct(k_low, count, skip, masked):
+        scores = [raw_scores(k_low, count, skip, h) for h in range(HEADS)]
+        probs = []
+        for h in range(HEADS):
+            weights = jnp.exp2(scores[h] * FACTOR)
+            if masked:
+                weights = jnp.where(allowed_pairs(k_low, count, skip), weights, 0.0)
+            probs.append(add(k_low, count, skip, h, weights))
+        for h in range(HEADS):
+            mix(k_low, count, skip, h, probs[h])
 
     def score(k_low, count, skip, masked):
-        keys = kv_ref[0, pl.ds(k_low, count), :]
-        if masked:
-            k_position = k_low + lax.broadcasted_iota(jnp.int32, (count, BQ - skip), 0)
-            allowed = (k_position >= first[:, skip:]) & (k_position <= position[:, skip:])
         for h in range(HEADS):
-            scores = jnp.dot(
-                keys, queries_t[h * HEAD : (h + 1) * HEAD, skip:],
-                preferred_element_type=jnp.float32,
-            )
+            scores = raw_scores(k_low, count, skip, h)
             if masked:
-                scores = jnp.where(allowed, scores, NEG)
+                scores = jnp.where(allowed_pairs(k_low, count, skip), scores, NEG)
             s_ref[h, pl.ds(k_low, count), skip:] = scores
             m_ref[h, :, skip:] = jnp.maximum(
                 m_ref[h, :, skip:], jnp.max(scores.reshape(count // 8, 8, BQ - skip), axis=0)
             )
 
-    def weigh(k_low, count, skip):
-        values = values_t[:, pl.ds(k_low, count)]
+    def weigh(k_low, count, skip, masked):
         for h in range(HEADS):
             scores = s_ref[h, pl.ds(k_low, count), skip:].reshape(count // 8, 8, BQ - skip)
             weights = jnp.exp2(scores * FACTOR - m_ref[h, :, skip:][None])
-            l_ref[h, :, skip:] += jnp.sum(weights, axis=0)
-            acc_ref[h, :, skip:] += jnp.dot(
-                values, weights.reshape(count, BQ - skip).astype(jnp.bfloat16),
-                preferred_element_type=jnp.float32,
-            )
+            mix(k_low, count, skip, h, add(k_low, count, skip, h, weights.reshape(count, BQ - skip)))
 
     half = BK // 2
     low = jnp.minimum(least // half, q_low // half)
     odd = (q_low // half - low) % 2
     whole = (q_low - (low + odd) * half) // BK
 
-    def each_block(act):
+    def all_blocks(act):
+        def ahead(k_low, count):
+            pl.when(k_low < most)(lambda: act(k_low, count, 0, True))
+            pl.when(k_low >= most)(lambda: act(k_low, count, 0, False))
+
         @pl.when(odd == 1)
         def _():
-            act(pl.multiple_of(low * half, half), half)
+            ahead(pl.multiple_of(low * half, half), half)
 
         @pl.loop(0, whole)
         def _(i):
-            act(pl.multiple_of((low + odd) * half + i * BK, half), BK)
-
-    def score_block(k_low, count):
-        pl.when(k_low < most)(lambda: score(k_low, count, 0, True))
-        pl.when(k_low >= most)(lambda: score(k_low, count, 0, False))
-
-    each_block(score_block)
-    score(q_low, half, 0, True)
-    score(pl.multiple_of(q_low + half, half), half, half, True)
-
-    for h in range(HEADS):
-        largest = jnp.max(m_ref[h], axis=0, keepdims=True) * FACTOR
-        m_ref[h] = jnp.broadcast_to(largest, (8, BQ))
-    l_ref[...] = jnp.zeros(l_ref.shape, jnp.float32)
-    acc_ref[...] = jnp.zeros(acc_ref.shape, jnp.float32)
-
-    each_block(lambda k_low, count: weigh(k_low, count, 0))
-    weigh(q_low, half, 0)
-    weigh(pl.multiple_of(q_low + half, half), half, half)
+            ahead(pl.multiple_of((low + odd) * half + i * BK, half), BK)
+
+        act(q_low, half, 0, True)
+        act(pl.multiple_of(q_low + half, half), half, half, True)
+
+    bound = jnp.max(jnp.abs(qg_ref[...])) * jnp.max(jnp.abs(kg_ref[...])) * SPREAD
+    in_range = bound <= EXPONENT_MOST
+
+    @pl.when(in_range)
+    def _():
+        all_blocks(direct)
+
+    @pl.when(jnp.logical_not(in_range))
+    def _():
+        m_ref[...] = jnp.full(m_ref.shape, NEG, jnp.float32)
+        all_blocks(score)
+        for h in range(HEADS):
+            largest = jnp.max(m_ref[h], axis=0, keepdims=True) * FACTOR
+            m_ref[h] = jnp.broadcast_to(largest, (8, BQ))
+        all_blocks(weigh)
 
     for h in range(HEADS):
         total = jnp.sum(l_ref[h], axis=0, keepdims=True)
@@ -432,7 +461,7 @@
         store_hid.wait()
 
 
-def attention(doc_lengths, queries, kv, hidden):
+def attention(doc_lengths, q_gain, k_gain, queries, kv, hidden):
     any_space = pl.BlockSpec(memory_space=pl.ANY)
     vmem = pltpu.VMEM
     f32, bf16 = jnp.float32, jnp.bfloat16
@@ -445,6 +474,8 @@
         ),
         in_specs=[
             pl.BlockSpec(memory_space=pltpu.SMEM),
+            pl.BlockSpec(memory_space=vmem),
+            pl.BlockSpec(memory_space=vmem),
             pl.BlockSpec((BQ, HEADS * HEAD), lambda i: (i, 0)),
             pl.BlockSpec((2, 3 * SHARD, HEAD), lambda i: (0, 0, 0)),
             any_space,
@@ -462,7 +493,7 @@
         ],
         compiler_params=pltpu.CompilerParams(vmem_limit_bytes=VMEM_LIMIT),
         name="attention",
-    )(doc_lengths, queries, kv, hidden)
+    )(doc_lengths, q_gain, k_gain, queries, kv, hidden)
 
 
 def per_device(
@@ -482,7 +513,12 @@
         key_gain.reshape(1, HEAD),
     )
     attended, hidden_out = attention(
-        doc_lengths, queries.reshape(SHARD, HEADS * HEAD), kv.reshape(2, 3 * SHARD, HEAD), hidden
+        doc_lengths,
+        query_gain.reshape(1, HEAD),
+        key_gain.reshape(1, HEAD),
+        queries.reshape(SHARD, HEADS * HEAD),
+        kv.reshape(2, 3 * SHARD, HEAD),
+        hidden,
     )
     return (hidden_out, attended)
 

time: 131 us -> 128 us (0.977)
  Pallas kernels: 130 us -> 127 us
    pallas_call x1, Pallas kernels: 20 us -> 17.5 us  [attention(): pl.pallas_call(attention_kernel, grid=(SHARD // BQ,), out_shape=(jax.Shap...]
where the time goes in v4:
time: 128 us
  Pallas kernels  127 us (99%)
    pallas_call x1, Pallas kernels, exchange(): pl.pallas_call(exchange_kernel, out_shape=(jax.ShapeDtypeStruct((TOK, MOD...  110 us
    pallas_call x1, Pallas kernels, attention(): pl.pallas_call(attention_kernel, grid=(SHARD // BQ,), out_shape=(jax.Shap...  17.5 us

profile of v4, /device:TPU:65, one launch (start us, length us, event | category | flops | bytes accessed | tf_op | source)
XLA Modules:
  0.0 127.8 jit_solution(14252335082608896701)
XLA Ops:
  0.6 109.5 %exchange.1 = (bf16[128,6400]{1,0:T(8,128)(2,1)}, bf16[8,8,16,640]{3,2,1,0:T(8,128)(2,1)}, bf16[2,3,8,8,16,128]{5,4,3,2,1,0:T(8,128)(2,1)}) custom-call(bf16[128,6400]{1,0:T(8,128)(2,1)} %res_hbm.1, bf16[128,6400]{1,0:T(8,128)(2,1)} %sh_hbm.1, bf16[8,32,6400]{2,1,0:T(8,128)(2,1)} %bitcast.13, s32[1,128]{1,0:T(1,128)} %bitcast.14, f32[1,128]{1,0:T(1,128)} %bitcast.15, ...), custom_call_target="tpu_custom_call" | custom-call | flops 10066329600 | bytes 16777216 | tf_op jit(solution)/shard_map/exchange/pallas_call | solution.py:275
  110.2 17.5 %attention.1 = (bf16[1024,640]{1,0:T(8,128)(2,1)}, bf16[128,6400]{1,0:T(8,128)(2,1)}) custom-call(s32[32]{0:T(128)} %doc_ref.1, f32[1,128]{1,0:T(1,128)} %bitcast.10, f32[1,128]{1,0:T(1,128)} %bitcast.12, bf16[1024,640]{1,0:T(8,128)(2,1)} %bitcast.8, bf16[2,3072,128]{2,1,0:T(8,128)(2,1)} %bitcast.7, bf16[128,6400]{1,0:T(8,128)(2,1)} %get-tuple-element.9.hid_hbm), custom_call_target="tpu_custom_call" | custom-call | tf_op jit(solution)/shard_map/attention/pallas_call | solution.py:468

commit v5 on v4

--- a/solution.py
+++ b/solution.py
@@ -330,7 +330,7 @@
 
 def attention_kernel(
     doc_ref, qg_ref, kg_ref, q_ref, kv_ref, hid_hbm, out_ref, hid_out_hbm, values_t, queries_t, s_ref, m_ref, l_ref,
-    acc_ref, hid, sem,
+    acc_ref, keep_ref, hid, sem,
 ):
     c = lax.axis_index("ctx")
     qb = pl.program_id(0)
@@ -383,18 +383,35 @@
             values_t[:, pl.ds(k_low, count)], probs, preferred_element_type=jnp.float32
         )
 
-    def direct(k_low, count, skip, masked):
-        scores = [raw_scores(k_low, count, skip, h) for h in range(HEADS)]
+    def direct(*parts):
+        at = 0
+        for k_low, count, skip, masked in parts:
+            if masked:
+                keep = jnp.where(allowed_pairs(k_low, count, skip), 1.0, 0.0)
+                keep_ref[at : at + count, skip:] = keep
+            at += count
+        scores = [
+            [raw_scores(k_low, count, skip, h) for h in range(HEADS)]
+            for k_low, count, skip, _ in parts
+        ]
         probs = []
-        for h in range(HEADS):
-            weights = jnp.exp2(scores[h] * FACTOR)
-            if masked:
-                weights = jnp.where(allowed_pairs(k_low, count, skip), weights, 0.0)
-            probs.append(add(k_low, count, skip, h, weights))
-        for h in range(HEADS):
-            mix(k_low, count, skip, h, probs[h])
-
-    def score(k_low, count, skip, masked):
+        at = 0
+        for i, (k_low, count, skip, masked) in enumerate(parts):
+            for h in range(HEADS):
+                weights = jnp.exp2(scores[i][h] * FACTOR)
+                if masked:
+                    weights = weights * keep_ref[at : at + count, skip:]
+                probs.append(add(k_low, count, skip, h, weights))
+            at += count
+        for i, (k_low, count, skip, _) in enumerate(parts):
+            for h in range(HEADS):
+                mix(k_low, count, skip, h, probs[i * HEADS + h])
+
+    def score(*parts):
+        for part in parts:
+            score_part(*part)
+
+    def score_part(k_low, count, skip, masked):
         for h in range(HEADS):
             scores = raw_scores(k_low, count, skip, h)
             if masked:
@@ -404,7 +421,11 @@
                 m_ref[h, :, skip:], jnp.max(scores.reshape(count // 8, 8, BQ - skip), axis=0)
             )
 
-    def weigh(k_low, count, skip, masked):
+    def weigh(*parts):
+        for part in parts:
+            weigh_part(*part)
+
+    def weigh_part(k_low, count, skip, masked):
         for h in range(HEADS):
             scores = s_ref[h, pl.ds(k_low, count), skip:].reshape(count // 8, 8, BQ - skip)
             weights = jnp.exp2(scores * FACTOR - m_ref[h, :, skip:][None])
@@ -417,8 +438,8 @@
 
     def all_blocks(act):
         def ahead(k_low, count):
-            pl.when(k_low < most)(lambda: act(k_low, count, 0, True))
-            pl.when(k_low >= most)(lambda: act(k_low, count, 0, False))
+            pl.when(k_low < most)(lambda: act((k_low, count, 0, True)))
+            pl.when(k_low >= most)(lambda: act((k_low, count, 0, False)))
 
         @pl.when(odd == 1)
         def _():
@@ -428,8 +449,7 @@
         def _(i):
             ahead(pl.multiple_of((low + odd) * half + i * BK, half), BK)
 
-        act(q_low, half, 0, True)
-        act(pl.multiple_of(q_low + half, half), half, half, True)
+        act((q_low, half, 0, True), (pl.multiple_of(q_low + half, half), half, half, True))
 
     bound = jnp.max(jnp.abs(qg_ref[...])) * jnp.max(jnp.abs(kg_ref[...])) * SPREAD
     in_range = bound <= EXPONENT_MOST
@@ -488,6 +508,7 @@
             vmem((HEADS, 8, BQ), f32),
             vmem((HEADS, 8, BQ), f32),
             vmem((HEADS, HEAD, BQ), f32),
+            vmem((BK, BQ), f32),
             vmem((TOK, MODEL), bf16),
             pltpu.SemaphoreType.DMA((2,)),
         ],

time: 128 us -> 131 us (1.023)
  Pallas kernels: 127 us -> 131 us
    pallas_call x1, Pallas kernels: 17.5 us -> 21.6 us  [attention(): pl.pallas_call(attention_kernel, grid=(SHARD // BQ,), out_shape=(jax.Shap...]
where the time goes in v5:
time: 131 us; the launch traced here: 132 us
  Pallas kernels  131 us (100%)
    pallas_call x1, Pallas kernels, exchange(): pl.pallas_call(exchange_kernel, out_shape=(jax.ShapeDtypeStruct((TOK, MOD...  110 us
    pallas_call x1, Pallas kernels, attention(): pl.pallas_call(attention_kernel, grid=(SHARD // BQ,), out_shape=(jax.Shap...  21.6 us

profile of v5, /device:TPU:65, one launch (start us, length us, event | category | flops | bytes accessed | tf_op | source)
XLA Modules:
  0.0 131.9 jit_solution(922224766641193888)
XLA Ops:
  0.6 109.5 %exchange.1 = (bf16[128,6400]{1,0:T(8,128)(2,1)}, bf16[8,8,16,640]{3,2,1,0:T(8,128)(2,1)}, bf16[2,3,8,8,16,128]{5,4,3,2,1,0:T(8,128)(2,1)}) custom-call(bf16[128,6400]{1,0:T(8,128)(2,1)} %res_hbm.1, bf16[128,6400]{1,0:T(8,128)(2,1)} %sh_hbm.1, bf16[8,32,6400]{2,1,0:T(8,128)(2,1)} %bitcast.13, s32[1,128]{1,0:T(1,128)} %bitcast.14, f32[1,128]{1,0:T(1,128)} %bitcast.15, ...), custom_call_target="tpu_custom_call" | custom-call | flops 10066329600 | bytes 16777216 | tf_op jit(solution)/shard_map/exchange/pallas_call | solution.py:275
  110.2 21.6 %attention.1 = (bf16[1024,640]{1,0:T(8,128)(2,1)}, bf16[128,6400]{1,0:T(8,128)(2,1)}) custom-call(s32[32]{0:T(128)} %doc_ref.1, f32[1,128]{1,0:T(1,128)} %bitcast.10, f32[1,128]{1,0:T(1,128)} %bitcast.12, bf16[1024,640]{1,0:T(8,128)(2,1)} %bitcast.8, bf16[2,3072,128]{2,1,0:T(8,128)(2,1)} %bitcast.7, bf16[128,6400]{1,0:T(8,128)(2,1)} %get-tuple-element.9.hid_hbm), custom_call_target="tpu_custom_call" | custom-call | tf_op jit(solution)/shard_map/attention/pallas_call | solution.py:488

commit v6 on v5

--- a/solution.py
+++ b/solution.py
@@ -247,10 +247,11 @@
                 qbuf[p, :, :, low + i * HEAD : low + (i + 1) * HEAD] = head.reshape(N_EXP, PR, HEAD)
         pltpu.make_async_copy(qbuf.at[p], q_hbm.at[:, p], out_sem.at[2]).start()
 
-        @pl.when(p > 0)
+        @pl.when(p > 1)
         def _():
-            pass_halo(p - 1)
-
+            pass_halo(p - 2)
+
+    pass_halo(PCH - 2)
     pass_halo(PCH - 1)
 
     done(ex_hbm.at[pl.ds(0, N_EXP - 1)], a_send)

time: 131 us -> 134 us (1.023)
  the two profiles are of different devices: /device:TPU:65 before, /device:TPU:3 now
where the time goes in v6:
time: 134 us; the launch traced here: 133 us
  Pallas kernels  133 us (99%)
    pallas_call x1, Pallas kernels, exchange(): pl.pallas_call(exchange_kernel, out_shape=(jax.ShapeDtypeStruct((TOK, MOD...  111 us
    pallas_call x1, Pallas kernels, attention(): pl.pallas_call(attention_kernel, grid=(SHARD // BQ,), out_shape=(jax.Shap...  21.6 us

profile of v6, /device:TPU:3, one launch (start us, length us, event | category | flops | bytes accessed | tf_op | source)
XLA Modules:
  0.0 133.3 jit_solution(16177257273365412355)
XLA Ops:
  0.6 111.0 %exchange.1 = (bf16[128,6400]{1,0:T(8,128)(2,1)}, bf16[8,8,16,640]{3,2,1,0:T(8,128)(2,1)}, bf16[2,3,8,8,16,128]{5,4,3,2,1,0:T(8,128)(2,1)}) custom-call(bf16[128,6400]{1,0:T(8,128)(2,1)} %res_hbm.1, bf16[128,6400]{1,0:T(8,128)(2,1)} %sh_hbm.1, bf16[8,32,6400]{2,1,0:T(8,128)(2,1)} %bitcast.13, s32[1,128]{1,0:T(1,128)} %bitcast.14, f32[1,128]{1,0:T(1,128)} %bitcast.15, ...), custom_call_target="tpu_custom_call" | custom-call | flops 10066329600 | bytes 16777216 | tf_op jit(solution)/shard_map/exchange/pallas_call | solution.py:276
  111.6 21.6 %attention.1 = (bf16[1024,640]{1,0:T(8,128)(2,1)}, bf16[128,6400]{1,0:T(8,128)(2,1)}) custom-call(s32[32]{0:T(128)} %doc_ref.1, f32[1,128]{1,0:T(1,128)} %bitcast.10, f32[1,128]{1,0:T(1,128)} %bitcast.12, bf16[1024,640]{1,0:T(8,128)(2,1)} %bitcast.8, bf16[2,3072,128]{2,1,0:T(8,128)(2,1)} %bitcast.7, bf16[128,6400]{1,0:T(8,128)(2,1)} %get-tuple-element.9.hid_hbm), custom_call_target="tpu_custom_call" | custom-call | tf_op jit(solution)/shard_map/attention/pallas_call | solution.py:489
